TPU v7x, 512 devices: a whole 4x8x8 slice. The times are simulated.
512 devices in a mesh: section: 4 (over x), space: 128 (over z, y, core).
Axes of the slice: x: 4, y: 8, z: 8, core: 2. Of those that a mesh axis runs over, the one named last changes fastest.
Arguments:
- grid_inputs: bfloat16 [2, 65536, 474], P(None, ('section', 'space')), may hold values from -6 to 6
- embed_weight: bfloat16 [474, 512], replicated, may hold values from -0.25 to 0.25
- embed_bias: float32 [512], replicated, may hold values from -3 to 3
- encode_weight: bfloat16 [512, 512], replicated, may hold values from -0.25 to 0.25
- encode_edge_weight: float32 [4, 512], replicated, may hold values from -3 to 3
- encode_bias: float32 [512], replicated, may hold values from -3 to 3
- mesh_gain: float32 [512], replicated, may hold values from 0.1 to 1.9
- process_weight: bfloat16 [4, 4, 512, 512], P('section'), may hold values from -0.25 to 0.25
- process_edge_weight: float32 [4, 4, 512], P('section'), may hold values from -3 to 3
- process_bias: float32 [4, 2, 512], P('section'), may hold values from -3 to 3
- process_gain: float32 [4, 512], P('section'), may hold values from 0.1 to 1.9
- decode_weight: bfloat16 [2, 512, 512], replicated, may hold values from -0.25 to 0.25
- decode_edge_weight: float32 [4, 512], replicated, may hold values from -3 to 3
- decode_bias: float32 [512], replicated, may hold values from -3 to 3
- output_weight: bfloat16 [512, 227], replicated, may hold values from -0.25 to 0.25
- encode_senders: int32 [4, 128, 192], P('section', 'space'), may hold values from 0 to 127, as said below
- encode_receivers: int32 [4, 128, 192], P('section', 'space'), may hold values from 0 to 128, as said below
- encode_features: float32 [4, 4, 128, 192], P(None, 'section', 'space'), may hold values from -6 to 6
- halo_send_rows: int32 [128, 64], P('space'), may hold values from 0 to 127, as said below
- mesh_senders: int32 [128, 448], P('space'), may hold values from 0 to 319, as said below
- mesh_receivers: int32 [128, 448], P('space'), may hold values from 0 to 127, as said below
- mesh_features: float32 [4, 128, 448], P(None, 'space'), may hold values from -6 to 6
- decode_senders: int32 [4, 128, 192], P('section', 'space'), may hold values from 0 to 127, as said below
- decode_receivers: int32 [4, 128, 192], P('section', 'space'), may hold values from 0 to 128, as said below
- decode_features: float32 [4, 4, 128, 192], P(None, 'section', 'space'), may hold values from -6 to 6
Outputs:
- forecast: bfloat16 [2, 65536, 227], P(None, ('section', 'space'))
Inputs may be any that keep to these rules, and one draw needn't show every extreme that they name: `encode_senders`: entry [s, q, i * 64 + k] is the local grid row that grid device (s, q) sends as its k-th row to mesh owner (s, (q + o_i) mod 128), o = (0, 1, -1). `encode_receivers`: entry [s, p, i * 64 + k] is the local mesh row of owner (s, p) that takes the k-th row from grid device (s, (p - o_i) mod 128); 128 marks an empty slot, used slots come first in each block of 64, and block 0 is full. `halo_send_rows`: entry [p, b * 16 + k] is the local mesh row that owner p sends to owner (p + h_b) mod 128 as its k-th halo row, h = (1, -1, 2, -2). `mesh_senders`: encoded as in the step on mesh edges; every value is used on every owner. `mesh_receivers`: the local mesh row that the edge updates; every row receives an edge. `decode_senders`: entry [s, p, i * 64 + k] is the local mesh row that owner (s, p) sends as its k-th row to grid device (s, (p + o_i) mod 128). `decode_receivers`: entry [s, q, i * 64 + k] is the local grid row of device (s, q) that takes the k-th row from mesh owner (s, (q - o_i) mod 128); 128 marks an empty slot, used slots come first in each block of 64, and block 0 is full.
All inputs are finite; a program needn't handle non-finite values.
Results may differ from a plain program's by a relative error of at most 0.018.
Values may be sent and summed in bfloat16 or wider, within the bound.
No kernel may reach another device: no remote copies, remote signals or barrier semaphores. Data moves between devices by JAX's collectives and lax.ppermute only.
A program may use at most 64 MiB of HBM per device.

v0:
```python
import jax
import jax.numpy as jnp
from jax import lax
from jax.sharding import PartitionSpec as P

M_DEV = 128
COARSE = 1


link_offsets = (0, 1, -1)
halo_offsets = (1, -1, 2, -2)


def shifted(x, axis, by):
    size = lax.axis_size(axis)
    return lax.ppermute(x, axis, [(i, (i + by) % size) for i in range(size)])


def from_behind(value, axis, steps):
    count = lax.axis_size(axis)
    leading, last = (max(0, -steps), min(count, count - steps))
    return lax.ppermute(value, axis, [(source, source + steps) for source in range(leading, last)])


def from_root(block, axis, owner):
    block = jnp.where(lax.axis_index(axis) == owner, block, jnp.zeros_like(block))
    return lax.psum(block, axis)


def edge_term(features, weight):
    running = features[0][:, None] * weight[0][None, :]
    for component in range(1, features.shape[0]):
        running = running + features[component][:, None] * weight[component][None, :]
    return running


def layer_norm(values, scales):
    center = values - jnp.mean(values, axis=-1, keepdims=True)
    spread = jnp.mean(center * center, axis=-1, keepdims=True)
    return center * lax.rsqrt(spread + 1e-05) * scales


def one_hot_rows(row_index, row_count):
    return (jnp.arange(row_count, dtype=jnp.int32)[:, None] == row_index[None, :]).astype(
        jnp.bfloat16
    )


def process(mesh_state, parameters, sources, targets, target_hot, send_rows):
    weights, edge_bias, node_bias, scales = parameters
    batch_size, row_count, latent = mesh_state.shape
    flattened = mesh_state.reshape(batch_size * row_count, latent)
    local_keys = jnp.dot(flattened, weights[0], preferred_element_type=jnp.float32).astype(
        jnp.bfloat16
    )
    local_keys = local_keys.reshape(batch_size, row_count, latent)
    target_keys = jnp.dot(flattened, weights[1], preferred_element_type=jnp.float32).astype(
        jnp.bfloat16
    )
    target_keys = target_keys.reshape(batch_size, row_count, latent)
    halo_count = send_rows.shape[0] // 4
    pieces = [local_keys]
    for position, offset in enumerate(halo_offsets):
        outgoing = local_keys[:, send_rows[position * halo_count : (position + 1) * halo_count], :]
        pieces.append(shifted(outgoing, "space", offset))
    pieces.append(lax.all_gather(local_keys[:, :COARSE, :], "space", axis=1, tiled=True))
    source_keys = jnp.concatenate(pieces, axis=1)
    summed_in = (
        source_keys[:, sources, :].astype(jnp.float32)
        + target_keys[:, targets, :].astype(jnp.float32)
        + edge_bias[None]
    )
    hidden = jax.nn.silu(summed_in).astype(jnp.bfloat16)
    node_in = jnp.einsum(
        "me,ked->kmd", target_hot, hidden, preferred_element_type=jnp.float32
    ).astype(jnp.bfloat16)
    update = jax.nn.silu(
        jnp.dot(
            node_in.reshape(batch_size * row_count, latent),
            weights[2],
            preferred_element_type=jnp.float32,
        )
        + jnp.dot(flattened, weights[3], preferred_element_type=jnp.float32)
        + node_bias
    )
    normed = layer_norm(update, scales).reshape(batch_size, row_count, latent)
    return (mesh_state.astype(jnp.float32) + normed).astype(jnp.bfloat16)


def shards(
    grid_inputs,
    embed_weight,
    embed_bias,
    encode_weight,
    encode_edge_weight,
    encode_bias,
    mesh_gain,
    process_weight,
    process_edge_weight,
    process_bias,
    process_gain,
    decode_weight,
    decode_edge_weight,
    decode_bias,
    output_weight,
    encode_senders,
    encode_receivers,
    encode_features,
    halo_send_rows,
    mesh_senders,
    mesh_receivers,
    mesh_features,
    decode_senders,
    decode_receivers,
    decode_features,
):
    samples, grid_rows, in_width = grid_inputs.shape
    latent = embed_weight.shape[1]
    link_count = encode_senders.shape[2] // 3
    flat_in = grid_inputs.reshape(samples * grid_rows, in_width)
    grid_latent = jax.nn.silu(
        jnp.dot(flat_in, embed_weight, preferred_element_type=jnp.float32) + embed_bias
    ).astype(jnp.bfloat16)
    grid_keys = jnp.dot(grid_latent, encode_weight, preferred_element_type=jnp.float32).astype(
        jnp.bfloat16
    )
    grid_keys = grid_keys.reshape(samples, grid_rows, latent)
    encode_list = encode_senders[0, 0]
    arrivals = []
    for position, offset in enumerate(link_offsets):
        outgoing = grid_keys[:, encode_list[position * link_count : (position + 1) * link_count], :]
        if offset == 0:
            arrivals.append(outgoing)
        else:
            arrivals.append(shifted(outgoing, "space", offset))
    arrived = jnp.concatenate(arrivals, axis=1)
    encode_edge = edge_term(encode_features[:, 0, 0, :], encode_edge_weight) + encode_bias
    message = jax.nn.silu(arrived.astype(jnp.float32) + encode_edge[None]).astype(jnp.bfloat16)
    partial_sums = jnp.einsum(
        "ms,ksd->kmd",
        one_hot_rows(encode_receivers[0, 0], M_DEV),
        message,
        preferred_element_type=jnp.float32,
    )
    totals = lax.psum(partial_sums, "section")
    mesh_start = layer_norm(totals, mesh_gain).astype(jnp.bfloat16)
    edge_features = mesh_features[:, 0, :]
    sources = mesh_senders[0]
    targets = mesh_receivers[0]
    send_rows = halo_send_rows[0]
    target_hot = one_hot_rows(targets, M_DEV)
    parameters = (
        process_weight[0],
        edge_term(edge_features, process_edge_weight[0]) + process_bias[0, 0],
        process_bias[0, 1],
        process_gain[0],
    )
    section_count = lax.axis_size("section")
    section_id = lax.axis_index("section")
    tick_count = section_count + samples - 1
    handed = jnp.zeros_like(mesh_start[0])
    finals = []
    for tick_index in range(tick_count):
        if tick_index < samples:
            layer_input = jnp.where(section_id == 0, mesh_start[tick_index], handed)
        else:
            layer_input = handed
        layer_output = process(
            layer_input[None], parameters, sources, targets, target_hot, send_rows
        )[0]
        if tick_index >= section_count - 1:
            finals.append(layer_output)
        if tick_index < tick_count - 1:
            handed = from_behind(layer_output, "section", 1)
    last_mesh = from_root(jnp.stack(finals), "section", section_count - 1)
    mesh_keys = (
        jnp.dot(
            last_mesh.reshape(samples * M_DEV, latent),
            decode_weight[0],
            preferred_element_type=jnp.float32,
        )
        .astype(jnp.bfloat16)
        .reshape(samples, M_DEV, latent)
    )
    decode_list = decode_senders[0, 0]
    deliveries = []
    for position, offset in enumerate(link_offsets):
        outgoing = mesh_keys[:, decode_list[position * link_count : (position + 1) * link_count], :]
        if offset == 0:
            deliveries.append(outgoing)
        else:
            deliveries.append(shifted(outgoing, "space", offset))
    arrived_mesh = jnp.concatenate(deliveries, axis=1)
    grid_queries = jnp.dot(
        grid_latent, decode_weight[1], preferred_element_type=jnp.float32
    ).astype(jnp.bfloat16)
    grid_queries = grid_queries.reshape(samples, grid_rows, latent)
    grid_targets = decode_receivers[0, 0]
    clamped = jnp.minimum(grid_targets, grid_rows - 1)
    decode_edge = edge_term(decode_features[:, 0, 0, :], decode_edge_weight) + decode_bias
    summed_in = (
        arrived_mesh.astype(jnp.float32)
        + grid_queries[:, clamped, :].astype(jnp.float32)
        + decode_edge[None]
    )
    hidden = jax.nn.silu(summed_in).astype(jnp.bfloat16)
    grid_sum = jnp.einsum(
        "gs,ksd->kgd",
        one_hot_rows(grid_targets, grid_rows),
        hidden,
        preferred_element_type=jnp.float32,
    ).astype(jnp.bfloat16)
    vars_count = output_weight.shape[1]
    change = jnp.dot(
        grid_sum.reshape(samples * grid_rows, latent),
        output_weight,
        preferred_element_type=jnp.float32,
    ).reshape(samples, grid_rows, vars_count)
    return (grid_inputs[:, :, :vars_count].astype(jnp.float32) + change).astype(jnp.bfloat16)


def solution(mesh):
    return jax.shard_map(
        shards,
        mesh=mesh,
        in_specs=(
            P(None, ("section", "space"), None),
            P(),
            P(),
            P(),
            P(),
            P(),
            P(),
            P("section", None, None, None),
            P("section", None, None),
            P("section", None, None),
            P("section", None),
            P(),
            P(),
            P(),
            P(),
            P("section", "space", None),
            P("section", "space", None),
            P(None, "section", "space", None),
            P("space", None),
            P("space", None),
            P("space", None),
            P(None, "space", None),
            P("section", "space", None),
            P("section", "space", None),
            P(None, "section", "space", None),
        ),
        out_specs=P(None, ("section", "space"), None),
        check_vma=False,
    )
```

profile of v0, /device:TPU:25, one launch (start us, length us, event | category | flops | bytes accessed | tf_op | source)
XLA Modules:
  0.0 580.2 jit_solution(11577991162958251167)
XLA Ops:
  11.8 5.0 collective-permute-start
  27.8 52.3 %all-reduce.3.cloned.1.call-done = f32[2,128,512]{1,2,0:T(8,128)} async-done(((f32[2,128,512]{1,2,0:T(8,128)}), f32[2,128,512]{1,2,0:T(8,128)}) %all-reduce.3.cloned.1.call-update) | async-done | bytes 524304 | tf_op jit(solution)/shard_map/psum | solution.py:145
  84.7 6.9 %collective-permute-start.2 = (bf16[1,16,512]{2,1,0:T(8,128)(2,1)S(1)}, bf16[1,16,512]{2,1,0:T(8,128)(2,1)}, u32[]{:S(2)}, u32[]{:S(2)}) collective-permute-start(bf16[1,16,512]{2,1,0:T(8,128)(2,1)S(1)} %bitcast.380), channel_id=1, source_target_pairs={{0,1},{1,2},{2,3},{3,4},{4,5},{5,6},{6,7},{7,8},{8,9},{9,10},{10,1... | collective-permute-start | bytes 49160 | tf_op jit(solution)/shard_map/ppermute | solution.py:16
  97.7 3.1 collective-permute-start.5
  103.4 53.5 %all_gather.15 = bf16[1,128,512]{2,0,1:T(2,128)(2,1)S(1)} all-gather(bf16[1,1,512]{2,0,1:T(2,128)(2,1)S(1)} %slice_bitcast_fusion.5), channel_id=1, replica_groups=mesh['section'=4,'space'=128] {'space'}, dimensions={1}, use_global_device_ids=true | all-gather | bytes 132096 | tf_op jit(solution)/shard_map/all_gather | solution.py:66
  168.0 2.7 collective-permute-done.6
  173.9 4.4 collective-permute-start.7
  182.5 3.1 collective-permute-start.10
  188.2 53.4 %all_gather.16 = bf16[1,128,512]{2,0,1:T(2,128)(2,1)S(1)} all-gather(bf16[1,1,512]{2,0,1:T(2,128)(2,1)S(1)} %slice_bitcast_fusion.4), channel_id=1, replica_groups=mesh['section'=4,'space'=128] {'space'}, dimensions={1}, use_global_device_ids=true | all-gather | bytes 132096 | tf_op jit(solution)/shard_map/all_gather | solution.py:66
  247.3 4.1 collective-permute-start.11
  257.2 3.1 collective-permute-start.12
  262.2 4.3 collective-permute-start.14
  271.3 54.8 %all_gather.17 = bf16[1,128,512]{2,0,1:T(2,128)(2,1)S(1)} all-gather(bf16[1,1,512]{2,0,1:T(2,128)(2,1)S(1)} %slice_bitcast_fusion.3), channel_id=1, replica_groups=mesh['section'=4,'space'=128] {'space'}, dimensions={1}, use_global_device_ids=true | all-gather | bytes 132096 | tf_op jit(solution)/shard_map/all_gather | solution.py:66
  331.7 4.1 collective-permute-start.16
  346.4 4.5 collective-permute-start.19
  355.6 54.6 %all_gather.18 = bf16[1,128,512]{2,0,1:T(2,128)(2,1)S(1)} all-gather(bf16[1,1,512]{2,0,1:T(2,128)(2,1)S(1)} %slice_bitcast_fusion.2), channel_id=1, replica_groups=mesh['section'=4,'space'=128] {'space'}, dimensions={1}, use_global_device_ids=true | all-gather | bytes 132096 | tf_op jit(solution)/shard_map/all_gather | solution.py:66
  416.2 4.1 collective-permute-start.21
  426.1 3.1 collective-permute-start.22
  431.1 4.3 collective-permute-start.24
  440.2 54.8 %all_gather.19 = bf16[1,128,512]{2,0,1:T(2,128)(2,1)S(1)} all-gather(bf16[1,1,512]{2,0,1:T(2,128)(2,1)S(1)} %slice_bitcast_fusion.1), channel_id=1, replica_groups=mesh['section'=4,'space'=128] {'space'}, dimensions={1}, use_global_device_ids=true | all-gather | bytes 132096 | tf_op jit(solution)/shard_map/all_gather | solution.py:66
  497.8 3.1 fusion.18
  506.2 47.8 %all-reduce.5.cloned.1.call-done = bf16[256,512]{1,0:T(8,128)(2,1)} async-done(((bf16[256,512]{1,0:T(8,128)(2,1)}), bf16[256,512]{1,0:T(8,128)(2,1)}) %all-reduce.5.cloned.1.call-update) | async-done | bytes 262160 | tf_op jit(solution)/shard_map/psum | solution.py:27
  556.6 7.0 %collective-permute-start.26 = (bf16[2,64,512]{2,1,0:T(8,128)(2,1)S(1)}, bf16[2,64,512]{2,1,0:T(8,128)(2,1)S(1)}, u32[]{:S(2)}, u32[]{:S(2)}) collective-permute-start(bf16[2,64,512]{2,1,0:T(8,128)(2,1)S(1)} %bitcast.355), channel_id=1, source_target_pairs={{0,1},{1,2},{2,3},{3,4},{4,5},{5,6},{6,7},{7,8},{8,9},{9,10},{10,1... | collective-permute-start | bytes 393224 | tf_op jit(solution)/shard_map/ppermute | solution.py:16
  567.6 4.4 collective-permute-done.27
  (315 shorter events, 122.6 us)
Async XLA Ops:
  6.5 73.6 %all-reduce.3.cloned.1.call-start = ((), (), s32[]{:S(2)}) async-start(), calls=%async_computation | async-start | bytes 1048576 | tf_op jit(solution)/shard_map/psum | solution.py:145
  11.8 10.9 %collective-permute-start = (bf16[2,64,512]{2,1,0:T(8,128)(2,1)S(1)}, bf16[2,64,512]{2,1,0:T(8,128)(2,1)S(1)}, u32[]{:S(2)}, u32[]{:S(2)}) collective-permute-start(bf16[2,64,512]{2,1,0:T(8,128)(2,1)S(1)} %bitcast.353), channel_id=1, source_target_pairs={{0,1},{1,2},{2,3},{3,4},{4,5},{5,6},{6,7},{7,8},{8,9},{9,10},{10,1... | collective-permute-start | bytes 393224 | tf_op jit(solution)/shard_map/ppermute | solution.py:16
  26.5 527.5 %all-reduce.5.cloned.1.call-start = ((), (), s32[]{:S(2)}) async-start(), calls=%async_computation.1 | async-start | bytes 524288 | tf_op jit(solution)/shard_map/psum | solution.py:27
  84.7 72.1 %collective-permute-start.2 = (bf16[1,16,512]{2,1,0:T(8,128)(2,1)S(1)}, bf16[1,16,512]{2,1,0:T(8,128)(2,1)}, u32[]{:S(2)}, u32[]{:S(2)}) collective-permute-start(bf16[1,16,512]{2,1,0:T(8,128)(2,1)S(1)} %bitcast.380), channel_id=1, source_target_pairs={{0,1},{1,2},{2,3},{3,4},{4,5},{5,6},{6,7},{7,8},{8,9},{9,10},{10,1... | collective-permute-start | bytes 49160 | tf_op jit(solution)/shard_map/ppermute | solution.py:16
  92.2 65.3 %collective-permute-start.3 = (bf16[1,16,512]{2,1,0:T(8,128)(2,1)S(1)}, bf16[1,16,512]{2,1,0:T(8,128)(2,1)}, u32[]{:S(2)}, u32[]{:S(2)}) collective-permute-start(bf16[1,16,512]{2,1,0:T(8,128)(2,1)S(1)} %bitcast.379), channel_id=1, source_target_pairs={{0,127},{1,0},{2,1},{3,2},{4,3},{5,4},{6,5},{7,6},{8,7},{9,8},{10,... | collective-permute-start | bytes 49160 | tf_op jit(solution)/shard_map/ppermute | solution.py:16
  94.8 63.5 %collective-permute-start.4 = (bf16[1,16,512]{2,1,0:T(8,128)(2,1)S(1)}, bf16[1,16,512]{2,1,0:T(8,128)(2,1)}, u32[]{:S(2)}, u32[]{:S(2)}) collective-permute-start(bf16[1,16,512]{2,1,0:T(8,128)(2,1)S(1)} %bitcast.378), channel_id=1, source_target_pairs={{0,2},{1,3},{2,4},{3,5},{4,6},{5,7},{6,8},{7,9},{8,10},{9,11},{10,... | collective-permute-start | bytes 49160 | tf_op jit(solution)/shard_map/ppermute | solution.py:16
  97.7 61.3 %collective-permute-start.5 = (bf16[1,16,512]{2,1,0:T(8,128)(2,1)S(1)}, bf16[1,16,512]{2,1,0:T(8,128)(2,1)}, u32[]{:S(2)}, u32[]{:S(2)}) collective-permute-start(bf16[1,16,512]{2,1,0:T(8,128)(2,1)S(1)} %bitcast.376), channel_id=1, source_target_pairs={{0,126},{1,127},{2,0},{3,1},{4,2},{5,3},{6,4},{7,5},{8,6},{9,7},{1... | collective-permute-start | bytes 49160 | tf_op jit(solution)/shard_map/ppermute | solution.py:16
  173.9 67.7 %collective-permute-start.7 = (bf16[1,16,512]{2,1,0:T(8,128)(2,1)S(1)}, bf16[1,16,512]{2,1,0:T(8,128)(2,1)S(1)}, u32[]{:S(2)}, u32[]{:S(2)}) collective-permute-start(bf16[1,16,512]{2,1,0:T(8,128)(2,1)S(1)} %bitcast.381), channel_id=1, source_target_pairs={{0,1},{1,2},{2,3},{3,4},{4,5},{5,6},{6,7},{7,8},{8,9},{9,10},{10,1... | collective-permute-start | bytes 49160 | tf_op jit(solution)/shard_map/ppermute | solution.py:16
  178.4 63.2 %collective-permute-start.8 = (bf16[1,16,512]{2,1,0:T(8,128)(2,1)S(1)}, bf16[1,16,512]{2,1,0:T(8,128)(2,1)S(1)}, u32[]{:S(2)}, u32[]{:S(2)}) collective-permute-start(bf16[1,16,512]{2,1,0:T(8,128)(2,1)S(1)} %bitcast.373), channel_id=1, source_target_pairs={{0,127},{1,0},{2,1},{3,2},{4,3},{5,4},{6,5},{7,6},{8,7},{9,8},{10,... | collective-permute-start | bytes 49160 | tf_op jit(solution)/shard_map/ppermute | solution.py:16
  180.3 61.3 %collective-permute-start.9 = (bf16[1,16,512]{2,1,0:T(8,128)(2,1)S(1)}, bf16[1,16,512]{2,1,0:T(8,128)(2,1)S(1)}, u32[]{:S(2)}, u32[]{:S(2)}) collective-permute-start(bf16[1,16,512]{2,1,0:T(8,128)(2,1)S(1)} %bitcast.369), channel_id=1, source_target_pairs={{0,2},{1,3},{2,4},{3,5},{4,6},{5,7},{6,8},{7,9},{8,10},{9,11},{10,... | collective-permute-start | bytes 49160 | tf_op jit(solution)/shard_map/ppermute | solution.py:16
  182.5 59.2 %collective-permute-start.10 = (bf16[1,16,512]{2,1,0:T(8,128)(2,1)S(1)}, bf16[1,16,512]{2,1,0:T(8,128)(2,1)S(1)}, u32[]{:S(2)}, u32[]{:S(2)}) collective-permute-start(bf16[1,16,512]{2,1,0:T(8,128)(2,1)S(1)} %bitcast.365), channel_id=1, source_target_pairs={{0,126},{1,127},{2,0},{3,1},{4,2},{5,3},{6,4},{7,5},{8,6},{9,7},{1... | collective-permute-start | bytes 49160 | tf_op jit(solution)/shard_map/ppermute | solution.py:16
  257.2 68.9 %collective-permute-start.12 = (bf16[1,16,512]{2,1,0:T(8,128)(2,1)S(1)}, bf16[1,16,512]{2,1,0:T(8,128)(2,1)S(1)}, u32[]{:S(2)}, u32[]{:S(2)}) collective-permute-start(bf16[1,16,512]{2,1,0:T(8,128)(2,1)S(1)} %bitcast.382), channel_id=1, source_target_pairs={{0,1},{1,2},{2,3},{3,4},{4,5},{5,6},{6,7},{7,8},{8,9},{9,10},{10,1... | collective-permute-start | bytes 49160 | tf_op jit(solution)/shard_map/ppermute | solution.py:16
  260.3 65.8 %collective-permute-start.13 = (bf16[1,16,512]{2,1,0:T(8,128)(2,1)S(1)}, bf16[1,16,512]{2,1,0:T(8,128)(2,1)S(1)}, u32[]{:S(2)}, u32[]{:S(2)}) collective-permute-start(bf16[1,16,512]{2,1,0:T(8,128)(2,1)S(1)} %bitcast.374), channel_id=1, source_target_pairs={{0,127},{1,0},{2,1},{3,2},{4,3},{5,4},{6,5},{7,6},{8,7},{9,8},{10,... | collective-permute-start | bytes 49160 | tf_op jit(solution)/shard_map/ppermute | solution.py:16
  262.2 63.9 %collective-permute-start.14 = (bf16[1,16,512]{2,1,0:T(8,128)(2,1)S(1)}, bf16[1,16,512]{2,1,0:T(8,128)(2,1)S(1)}, u32[]{:S(2)}, u32[]{:S(2)}) collective-permute-start(bf16[1,16,512]{2,1,0:T(8,128)(2,1)S(1)} %bitcast.370), channel_id=1, source_target_pairs={{0,2},{1,3},{2,4},{3,5},{4,6},{5,7},{6,8},{7,9},{8,10},{9,11},{10,... | collective-permute-start | bytes 49160 | tf_op jit(solution)/shard_map/ppermute | solution.py:16
  266.5 59.6 %collective-permute-start.15 = (bf16[1,16,512]{2,1,0:T(8,128)(2,1)S(1)}, bf16[1,16,512]{2,1,0:T(8,128)(2,1)S(1)}, u32[]{:S(2)}, u32[]{:S(2)}) collective-permute-start(bf16[1,16,512]{2,1,0:T(8,128)(2,1)S(1)} %bitcast.366), channel_id=1, source_target_pairs={{0,126},{1,127},{2,0},{3,1},{4,2},{5,3},{6,4},{7,5},{8,6},{9,7},{1... | collective-permute-start | bytes 49160 | tf_op jit(solution)/shard_map/ppermute | solution.py:16
  341.6 68.7 %collective-permute-start.17 = (bf16[1,16,512]{2,1,0:T(8,128)(2,1)S(1)}, bf16[1,16,512]{2,1,0:T(8,128)(2,1)S(1)}, u32[]{:S(2)}, u32[]{:S(2)}) collective-permute-start(bf16[1,16,512]{2,1,0:T(8,128)(2,1)S(1)} %bitcast.383), channel_id=1, source_target_pairs={{0,1},{1,2},{2,3},{3,4},{4,5},{5,6},{6,7},{7,8},{8,9},{9,10},{10,1... | collective-permute-start | bytes 49160 | tf_op jit(solution)/shard_map/ppermute | solution.py:16
  344.3 66.0 %collective-permute-start.18 = (bf16[1,16,512]{2,1,0:T(8,128)(2,1)S(1)}, bf16[1,16,512]{2,1,0:T(8,128)(2,1)S(1)}, u32[]{:S(2)}, u32[]{:S(2)}) collective-permute-start(bf16[1,16,512]{2,1,0:T(8,128)(2,1)S(1)} %bitcast.375), channel_id=1, source_target_pairs={{0,127},{1,0},{2,1},{3,2},{4,3},{5,4},{6,5},{7,6},{8,7},{9,8},{10,... | collective-permute-start | bytes 49160 | tf_op jit(solution)/shard_map/ppermute | solution.py:16
  346.4 63.9 %collective-permute-start.19 = (bf16[1,16,512]{2,1,0:T(8,128)(2,1)S(1)}, bf16[1,16,512]{2,1,0:T(8,128)(2,1)S(1)}, u32[]{:S(2)}, u32[]{:S(2)}) collective-permute-start(bf16[1,16,512]{2,1,0:T(8,128)(2,1)S(1)} %bitcast.371), channel_id=1, source_target_pairs={{0,2},{1,3},{2,4},{3,5},{4,6},{5,7},{6,8},{7,9},{8,10},{9,11},{10,... | collective-permute-start | bytes 49160 | tf_op jit(solution)/shard_map/ppermute | solution.py:16
  350.9 59.5 %collective-permute-start.20 = (bf16[1,16,512]{2,1,0:T(8,128)(2,1)S(1)}, bf16[1,16,512]{2,1,0:T(8,128)(2,1)S(1)}, u32[]{:S(2)}, u32[]{:S(2)}) collective-permute-start(bf16[1,16,512]{2,1,0:T(8,128)(2,1)S(1)} %bitcast.367), channel_id=1, source_target_pairs={{0,126},{1,127},{2,0},{3,1},{4,2},{5,3},{6,4},{7,5},{8,6},{9,7},{1... | collective-permute-start | bytes 49160 | tf_op jit(solution)/shard_map/ppermute | solution.py:16
  426.1 68.9 %collective-permute-start.22 = (bf16[1,16,512]{2,1,0:T(8,128)(2,1)S(1)}, bf16[1,16,512]{2,1,0:T(8,128)(2,1)S(1)}, u32[]{:S(2)}, u32[]{:S(2)}) collective-permute-start(bf16[1,16,512]{2,1,0:T(8,128)(2,1)S(1)} %bitcast.377), channel_id=1, source_target_pairs={{0,1},{1,2},{2,3},{3,4},{4,5},{5,6},{6,7},{7,8},{8,9},{9,10},{10,1... | collective-permute-start | bytes 49160 | tf_op jit(solution)/shard_map/ppermute | solution.py:16
  429.2 65.8 %collective-permute-start.23 = (bf16[1,16,512]{2,1,0:T(8,128)(2,1)S(1)}, bf16[1,16,512]{2,1,0:T(8,128)(2,1)S(1)}, u32[]{:S(2)}, u32[]{:S(2)}) collective-permute-start(bf16[1,16,512]{2,1,0:T(8,128)(2,1)S(1)} %bitcast.372), channel_id=1, source_target_pairs={{0,127},{1,0},{2,1},{3,2},{4,3},{5,4},{6,5},{7,6},{8,7},{9,8},{10,... | collective-permute-start | bytes 49160 | tf_op jit(solution)/shard_map/ppermute | solution.py:16
  431.1 63.9 %collective-permute-start.24 = (bf16[1,16,512]{2,1,0:T(8,128)(2,1)S(1)}, bf16[1,16,512]{2,1,0:T(8,128)(2,1)S(1)}, u32[]{:S(2)}, u32[]{:S(2)}) collective-permute-start(bf16[1,16,512]{2,1,0:T(8,128)(2,1)S(1)} %bitcast.368), channel_id=1, source_target_pairs={{0,2},{1,3},{2,4},{3,5},{4,6},{5,7},{6,8},{7,9},{8,10},{9,11},{10,... | collective-permute-start | bytes 49160 | tf_op jit(solution)/shard_map/ppermute | solution.py:16
  435.4 59.6 %collective-permute-start.25 = (bf16[1,16,512]{2,1,0:T(8,128)(2,1)S(1)}, bf16[1,16,512]{2,1,0:T(8,128)(2,1)S(1)}, u32[]{:S(2)}, u32[]{:S(2)}) collective-permute-start(bf16[1,16,512]{2,1,0:T(8,128)(2,1)S(1)} %bitcast.364), channel_id=1, source_target_pairs={{0,126},{1,127},{2,0},{3,1},{4,2},{5,3},{6,4},{7,5},{8,6},{9,7},{1... | collective-permute-start | bytes 49160 | tf_op jit(solution)/shard_map/ppermute | solution.py:16
  556.6 11.0 %collective-permute-start.26 = (bf16[2,64,512]{2,1,0:T(8,128)(2,1)S(1)}, bf16[2,64,512]{2,1,0:T(8,128)(2,1)S(1)}, u32[]{:S(2)}, u32[]{:S(2)}) collective-permute-start(bf16[2,64,512]{2,1,0:T(8,128)(2,1)S(1)} %bitcast.355), channel_id=1, source_target_pairs={{0,1},{1,2},{2,3},{3,4},{4,5},{5,6},{6,7},{7,8},{8,9},{9,10},{10,1... | collective-permute-start | bytes 393224 | tf_op jit(solution)/shard_map/ppermute | solution.py:16
  (64 other events, 712.6 us)
Sparse Core Ops, SparseCore 0:
  26.6 53.4 all-reduce.2
  503.5 50.4 all-reduce.4
where the time goes:
time: 582 us; the launch traced here: 580 us
  blocking collectives  271 us (47%)
  waiting for transfers between devices  117 us (20%)
  starting transfers between devices  89.7 us (15%)
  local copies, waits for them, and re-layouts  56.2 us (10%)
  matrix products  24 us (4%)
  between operations  15.2 us (3%)
  other arithmetic  7.22 us (1%)
    all_gather x5, blocking collectives, process(): lax.all_gather(local_keys[:, :COARSE, :], 'space', axis=1, tiled=True)  271 us
    ppermute x24, starting transfers between devices, shifted(): return lax.ppermute(x, axis, [(i, (i + by) % size) for i in range(size)])  75.1 us
    psum x1, waiting for transfers between devices, shards(): totals = lax.psum(partial_sums, 'section')  52.3 us
    psum x1, waiting for transfers between devices, from_root(): return lax.psum(block, axis)  47.8 us
    ppermute x4, starting transfers between devices, from_behind(): lax.ppermute(value, axis, [(source, source + steps) for source in range(l...  14.5 us
    gather x20, local copies, waits for them, and re-layouts, process(): local_keys[:, send_rows[position * halo_count:(position + 1) * halo_count...  13.4 us
    gather x5, local copies, waits for them, and re-layouts, process(): source_keys[:, sources, :].astype(jnp.float32)  13 us
    gather x5, local copies, waits for them, and re-layouts, process(): target_keys[:, targets, :].astype(jnp.float32)  13 us
  transfers between devices with their start and end apart: 30, of which 8 were waited for; matrix products, arithmetic and copies ran while one was open for 5% of the time, Pallas kernels for 0%

commit v1 on v0

v1 whole, which is shorter than its diff:
```python
import functools

import jax
import jax.numpy as jnp
from jax import lax
from jax.experimental import pallas as pl
from jax.experimental.pallas import tpu as pltpu
from jax.sharding import PartitionSpec as P

BF = jnp.bfloat16
F32 = jnp.float32
ROWS = 128
HALO = 16
EXTRA = 64
NODE_BIAS, GAIN = 32, 35
VMEM_LIMIT = 24 * 1024 * 1024


def silu(v):
    return v * (0.5 + 0.5 * jnp.tanh(0.5 * v))


def dot(a, b):
    return jnp.dot(a, b, preferred_element_type=F32)


def dot_t(a, b):
    return lax.dot_general(a, b, (((0,), (0,)), ((), ())), preferred_element_type=F32)


def split3(x):
    hi = x.astype(BF)
    rest = x - hi.astype(F32)
    mid = rest.astype(BF)
    low = (rest - mid.astype(F32)).astype(BF)
    return hi, mid, low


def layer_norm(values, gain):
    center = values - jnp.mean(values, axis=-1, keepdims=True)
    spread = jnp.mean(center * center, axis=-1, keepdims=True)
    return center * lax.rsqrt(spread + 1e-05) * gain


def hot_rows(index_row, count):
    n = index_row.shape[1]
    return (lax.broadcasted_iota(jnp.int32, (count, n), 0) == index_row).astype(F32).astype(BF)


def feature_parts(features):
    hi, mid, low = split3(features)
    return jnp.concatenate([p.astype(F32) for p in (hi, hi, mid, mid, hi, low)], axis=0)


def weight_parts(weight):
    hi, mid, low = split3(weight)
    return jnp.concatenate([p.astype(F32) for p in (hi, mid, hi, mid, low, hi)], axis=0)


def edge_term(features, weight):
    return dot_t(feature_parts(features).astype(BF), weight_parts(weight).astype(BF))


def call(kernel, out, *args, smem=0, hbm=0, scratch=(), hbm_out=False, cost=1_000_000):
    count = len(args)
    specs = []
    for position in range(count):
        if position < smem:
            specs.append(pl.BlockSpec(memory_space=pltpu.SMEM))
        elif position >= count - hbm:
            specs.append(pl.BlockSpec(memory_space=pl.ANY))
        else:
            specs.append(pl.BlockSpec(memory_space=pltpu.VMEM))
    out_spec = pl.BlockSpec(memory_space=pl.ANY if hbm_out else pltpu.VMEM)
    return pl.pallas_call(
        kernel,
        out_shape=out,
        in_specs=specs,
        out_specs=jax.tree.map(lambda _: out_spec, out),
        scratch_shapes=list(scratch),
        compiler_params=pltpu.CompilerParams(vmem_limit_bytes=VMEM_LIMIT),
        cost_estimate=pl.CostEstimate(flops=cost, bytes_accessed=1_000_000, transcendentals=0),
    )(*args)


def shape(dims, dtype=BF):
    return jax.ShapeDtypeStruct(dims, dtype)


def pack_weights_kernel(core, edge_weight, bias, gain, weight, out, extras, sems):
    half = 2 * weight.shape[1]
    first = [
        pltpu.make_async_copy(
            weight.at[2 * core[0] + m],
            out.at[pl.ds(m * (half // 2), half // 2)],
            sems.at[m],
        )
        for m in range(2)
    ]
    for copy in first:
        copy.start()
    width = edge_weight.shape[1]
    b_parts = [p.astype(F32) for p in split3(bias[0:1, :])]
    n_parts = [p.astype(F32) for p in split3(bias[1:2, :])]
    g_parts = [p.astype(F32) for p in split3(gain[...])]
    rows = jnp.concatenate(
        [weight_parts(edge_weight[...])]
        + b_parts
        + [jnp.zeros((5, width), F32)]
        + n_parts
        + g_parts
        + [jnp.zeros((EXTRA - 38, width), F32)],
        axis=0,
    )
    extras[...] = rows.astype(BF)
    tail = pltpu.make_async_copy(extras, out.at[pl.ds(half, EXTRA)], sems.at[2])
    tail.start()
    for copy in first:
        copy.wait()
    tail.wait()


def setup_kernel(meta, edges_out, sums_out, halo_out, *, coarse):
    edges = sums_out.shape[2]
    padded = -(-edges // 128) * 128
    table = edges_out.shape[2]
    target_at = ROWS + 4 * HALO + coarse
    extra_at = target_at + ROWS
    for owner in range(2):
        senders = meta[owner, 0:1, :].astype(jnp.int32)
        receivers = meta[owner, 1:2, :].astype(jnp.int32)
        pad = padded - edges
        features = meta[owner, 4:8, :]
        if pad:
            senders = jnp.concatenate([senders, jnp.full((1, pad), -1, jnp.int32)], axis=1)
            receivers_wide = jnp.concatenate([receivers, jnp.full((1, pad), -1000, jnp.int32)], axis=1)
            features = jnp.concatenate([features, jnp.zeros((4, pad), F32)], axis=1)
        else:
            receivers_wide = receivers
        row = lax.broadcasted_iota(jnp.int32, (extra_at, padded), 0)
        hot = ((row == senders) | (row == receivers_wide + target_at)).astype(F32)
        tail = jnp.concatenate(
            [
                feature_parts(features),
                jnp.ones((3, padded), F32),
                jnp.zeros((EXTRA - 27, padded), F32),
            ],
            axis=0,
        )
        whole = jnp.concatenate([hot, tail], axis=0)
        edges_out[owner] = jnp.transpose(whole)[:edges].astype(BF)
        sums_out[owner] = hot_rows(receivers, ROWS)
    sent = (meta[0, 2:3, 0 : 8 * HALO] + meta[1, 2:3, 0 : 8 * HALO]).astype(jnp.int32)
    hot = (lax.broadcasted_iota(jnp.int32, (2 * ROWS, 8 * HALO), 0) == sent).astype(F32)
    halo_out[...] = jnp.transpose(hot).astype(BF)


def embed_kernel(core, x, embed_weight, embed_bias, encode_weight, query_weight, senders, own, near, far, queries):
    latent = silu(dot(x[...], embed_weight[...]) + embed_bias[...]).astype(BF)
    keys = dot(latent, encode_weight[...]).astype(BF)
    send_blocks(core, keys, senders, own, near, far)
    queries[...] = dot(latent, query_weight[...]).astype(BF)


def send_blocks(core, keys, senders, own, near, far):
    first = core[0] == 0
    cap = senders.shape[1] // 3
    hot = hot_rows(senders[...], ROWS)
    for sample in range(2):
        rows = dot_t(hot, keys[sample * ROWS : (sample + 1) * ROWS]).astype(BF)
        out = pl.ds(sample * cap, cap)
        own[out] = rows[:cap]
        near[out] = jnp.where(first, rows[cap : 2 * cap], rows[2 * cap :])
        far[out] = jnp.where(first, rows[2 * cap :], rows[cap : 2 * cap])


def arrived_rows(core, own, near, far, sample):
    first = core[0] == 0
    cap = own.shape[0] // 2
    at = pl.ds(sample * cap, cap)
    from_near = jnp.where(first, near[1, at], near[0, at])
    from_far = far[at]
    return jnp.concatenate(
        [own[at], jnp.where(first, from_far, from_near), jnp.where(first, from_near, from_far)],
        axis=0,
    ).astype(F32)


def message_kernel(core, own, near, far, features, weight, bias, receivers, out):
    edge = edge_term(features[...], weight[...]) + bias[...]
    hot = hot_rows(receivers[...], ROWS)
    for sample in range(2):
        rows = arrived_rows(core, own, near, far, sample)
        message = silu(rows + edge).astype(BF)
        sums = dot(hot, message).astype(BF)
        out[sample] = sums
        out[sample + 2] = sums


def start_kernel(parts, gain, out):
    total = parts[0].astype(F32)
    for section in range(1, parts.shape[0]):
        total = total + parts[section].astype(F32)
    out[...] = layer_norm(total, gain[...]).astype(BF)


def outgoing(core, state, halo_hot, coarse_out, halo_out, inner_out):
    rows = dot(halo_hot[...], state).astype(BF)
    halo_out[...] = jnp.where(core[0] == 0, rows[3 * HALO : 6 * HALO], rows[: 3 * HALO])
    inner_out[...] = rows[6 * HALO :]
    pair = jnp.concatenate([state[0:1].astype(F32), state[ROWS : ROWS + 1].astype(F32)], axis=0)
    coarse_out[...] = jnp.broadcast_to(pair.astype(BF)[None], coarse_out.shape)


def prepare_kernel(core, state, halo_hot, coarse_out, halo_out, inner_out):
    outgoing(core, state[...], halo_hot, coarse_out, halo_out, inner_out)


def layer_body(state, halo, inner, coarse, edges_hot, sums_hot, wbuf, ebuf, sources, table, waits):
    coarse_rows = coarse.shape[0]
    at_halo = 2 * ROWS
    at_inner = at_halo + 6 * HALO
    at_coarse = at_inner + 2 * HALO
    sources[0:at_halo] = state[...]
    sources[at_halo : at_halo + 3 * HALO] = halo[0]
    sources[at_halo + 3 * HALO : at_inner] = halo[1]
    sources[at_inner:at_coarse] = inner[...]
    sources[at_coarse : at_coarse + coarse_rows] = coarse[...]
    waits[0].wait()
    keys = dot(sources[...], wbuf[0]).astype(BF)
    waits[1].wait()
    target = dot(state[...], wbuf[1]).astype(BF)
    up, down = at_halo, at_halo + 3 * HALO
    halo_from = (
        (up + HALO, at_inner, up, down + HALO),
        (at_inner + HALO, down, up + 2 * HALO, down + 2 * HALO),
    )
    at_target = ROWS + 4 * HALO + coarse_rows
    waits[4].wait()
    nodes = []
    for owner in range(2):
        table[0:ROWS] = keys[owner * ROWS : (owner + 1) * ROWS]
        for block in range(4):
            source = halo_from[owner][block]
            table[ROWS + block * HALO : ROWS + (block + 1) * HALO] = keys[source : source + HALO]
        table[ROWS + 4 * HALO : at_target] = keys[at_coarse : at_coarse + coarse_rows]
        table[at_target : at_target + ROWS] = target[owner * ROWS : (owner + 1) * ROWS]
        table[at_target + ROWS :] = ebuf[...]
        hidden = silu(dot(edges_hot[owner], table[...])).astype(BF)
        nodes.append(dot(sums_hot[owner], hidden).astype(BF))
    node_in = jnp.concatenate(nodes, axis=0)
    waits[2].wait()
    waits[3].wait()

    def vector(at):
        return (ebuf[at : at + 1].astype(F32) + ebuf[at + 1 : at + 2].astype(F32)) + ebuf[
            at + 2 : at + 3
        ].astype(F32)

    update = silu(dot(node_in, wbuf[2]) + dot(state[...], wbuf[3]) + vector(NODE_BIAS))
    return (state[...].astype(F32) + layer_norm(update, vector(GAIN))).astype(BF)


def fetch(core, wbuf, ebuf, sems, mine, other, use_own=None, own=None, own_half=None):
    size = wbuf.shape[1]

    def from_half(half, m):
        return half.at[pl.ds((m % 2) * size, size)]

    got = None if use_own is None else jnp.logical_not(use_own)

    def both(condition):
        return condition if got is None else jnp.logical_and(got, condition)

    waits = []
    for m in range(4):
        if use_own is not None:

            @pl.when(use_own)
            def _(m=m):
                pltpu.make_async_copy(own.at[m], wbuf.at[m], sems.at[m]).start()

        @pl.when(both(core[0] == m // 2))
        def _(m=m):
            pltpu.make_async_copy(from_half(mine, m), wbuf.at[m], sems.at[m]).start()

        @pl.when(both(core[0] != m // 2))
        def _(m=m):
            pltpu.make_async_copy(from_half(other, m), wbuf.at[m], sems.at[m]).start()

        waits.append(pltpu.make_async_copy(from_half(mine, m), wbuf.at[m], sems.at[m]))
    tail = pl.ds(2 * size, EXTRA)
    if use_own is not None:

        @pl.when(use_own)
        def _():
            pltpu.make_async_copy(own_half.at[tail], ebuf, sems.at[4]).start()

        @pl.when(got)
        def _():
            pltpu.make_async_copy(mine.at[tail], ebuf, sems.at[4]).start()

    else:
        pltpu.make_async_copy(mine.at[tail], ebuf, sems.at[4]).start()
    waits.append(pltpu.make_async_copy(mine.at[tail], ebuf, sems.at[4]))
    return waits


def early_layer_kernel(
    core, state, halo, inner, coarse, edges_hot, sums_hot, halo_hot, own, own_half, mine, other,
    state_out, coarse_out, halo_out, inner_out, wbuf, ebuf, sources, table, sems, *, layer,
):
    waits = fetch(core, wbuf, ebuf, sems, mine, other, core[1] == layer, own, own_half)
    new = layer_body(state, halo, inner, coarse, edges_hot, sums_hot, wbuf, ebuf, sources, table, waits)
    state_out[...] = new
    outgoing(core, new, halo_hot, coarse_out, halo_out, inner_out)


def late_layer_kernel(
    core, state, halo, inner, coarse, edges_hot, sums_hot, halo_hot, mine, other,
    state_out, coarse_out, halo_out, inner_out, wbuf, ebuf, sources, table, sems, *, layer,
):
    waits = fetch(core, wbuf, ebuf, sems, mine.at[layer], other.at[layer - 2])
    new = layer_body(state, halo, inner, coarse, edges_hot, sums_hot, wbuf, ebuf, sources, table, waits)
    state_out[...] = new
    outgoing(core, new, halo_hot, coarse_out, halo_out, inner_out)


def last_layer_kernel(
    core, state, halo, inner, coarse, edges_hot, sums_hot, decode, mine, other,
    keys_out, wbuf, ebuf, sources, table, sems, *, layer,
):
    waits = fetch(core, wbuf, ebuf, sems, mine.at[layer], other.at[layer - 2])
    new = layer_body(state, halo, inner, coarse, edges_hot, sums_hot, wbuf, ebuf, sources, table, waits)
    own = jnp.where(core[0] == 0, new[:ROWS], new[ROWS:])
    keys = dot(own, decode[...]).astype(BF)
    for section in range(keys_out.shape[0]):
        keys_out[section] = keys


def deliver_kernel(core, keys, senders, own, near, far):
    both = jnp.concatenate([keys[0], keys[1]], axis=0)
    send_blocks(core, both, senders, own, near, far)


def decode_kernel(core, own, near, far, queries, features, weight, bias, receivers, x, out_weight, out):
    edge = edge_term(features[...], weight[...]) + bias[...]
    hot = hot_rows(receivers[...], ROWS)
    width = out_weight.shape[1]
    for sample in range(2):
        at = pl.ds(sample * ROWS, ROWS)
        rows = arrived_rows(core, own, near, far, sample)
        hidden = silu(rows + dot_t(hot, queries[at]) + edge).astype(BF)
        total = dot(hot, hidden).astype(BF)
        change = dot(total, out_weight[...])
        out[sample] = (x[at, :width].astype(F32) + change).astype(BF)


def shards(
    grid_inputs, embed_weight, embed_bias, encode_weight, encode_edge_weight, encode_bias, mesh_gain,
    process_weight, process_edge_weight, process_bias, process_gain, decode_weight, decode_edge_weight,
    decode_bias, output_weight, encode_senders, encode_receivers, encode_features, halo_send_rows,
    mesh_senders, mesh_receivers, mesh_features, decode_senders, decode_receivers, decode_features,
):
    samples, grid_rows, in_width = grid_inputs.shape
    latent = embed_weight.shape[1]
    owners = lax.axis_size("space")
    chips = owners // 2
    sections = lax.axis_size("section")
    section = lax.axis_index("section")
    core_id = lax.axis_index("space") % 2
    core = jnp.stack([core_id, section % 2]).astype(jnp.int32)
    pairs = [[2 * k, 2 * k + 1] for k in range(chips)]
    same_core = [[2 * k + c for k in range(chips)] for c in range(2)]
    to_neighbour = [(2 * k + 1, (2 * k + 2) % owners) for k in range(chips)] + [
        (2 * k, (2 * k - 1) % owners) for k in range(chips)
    ]
    swap = [(i, i ^ 1) for i in range(owners)]

    def gather_pair(value):
        return lax.all_gather(value, "space", axis=0, axis_index_groups=pairs)

    def to_next(value):
        return lax.ppermute(value, "space", to_neighbour)

    def vec(value):
        return value.reshape(1, -1)

    half_rows = 2 * latent + EXTRA
    half = call(
        pack_weights_kernel,
        shape((half_rows, latent)),
        core, process_edge_weight[0], process_bias[0], process_gain, process_weight[0],
        smem=1, hbm=1, hbm_out=True,
        scratch=[pltpu.VMEM((EXTRA, latent), BF), pltpu.SemaphoreType.DMA((3,))],
    )
    partner = lax.ppermute(half, "section", [(i, i ^ 1) for i in range(sections)])

    x = grid_inputs.reshape(samples * grid_rows, in_width)
    cap = encode_senders.shape[2] // 3
    block = shape((samples * cap, latent))
    own, near, far, queries = call(
        embed_kernel,
        (block, block, block, shape((samples * grid_rows, latent))),
        core, x, embed_weight, vec(embed_bias), encode_weight, decode_weight[1], encode_senders[0],
        smem=1,
    )
    far = to_next(far)
    near = gather_pair(near)
    edges = mesh_senders.shape[1]
    b = halo_send_rows.reshape(4, HALO)
    none = jnp.zeros((HALO,), jnp.int32)
    low = jnp.concatenate([b[2], none, none, b[1], b[3], none, none, b[0]])
    high = jnp.concatenate([none, b[0] + ROWS, b[2] + ROWS, none, none, b[3] + ROWS, b[1] + ROWS, none])
    halo_list = jnp.pad(jnp.where(core_id == 0, low, high), (0, edges - 8 * HALO))
    meta = jnp.concatenate(
        [
            jnp.stack([mesh_senders[0], mesh_receivers[0], halo_list, jnp.zeros_like(halo_list)]).astype(F32),
            mesh_features[:, 0, :],
        ],
        axis=0,
    )
    meta = gather_pair(meta)
    table_rows = 2 * ROWS + 4 * HALO + owners + EXTRA
    edges_hot, sums_hot, halo_hot = call(
        functools.partial(setup_kernel, coarse=owners),
        (shape((2, edges, table_rows)), shape((2, ROWS, edges)), shape((8 * HALO, 2 * ROWS))),
        meta,
    )
    parts = call(
        message_kernel,
        shape((sections, ROWS, latent)),
        core, own, near, far, encode_features[:, 0, 0, :], encode_edge_weight, vec(encode_bias), encode_receivers[0],
        smem=1,
    )
    parts = lax.all_to_all(parts, "section", 0, 0, tiled=True)
    start = call(start_kernel, shape((ROWS, latent)), parts, vec(mesh_gain))
    state = gather_pair(start).reshape(2 * ROWS, latent)

    partner_other = lax.ppermute(partner, "space", swap)
    sent_half = lax.optimization_barrier((half, partner))[0]
    gathered = lax.all_gather(sent_half, "section", axis=0)
    gathered_other = lax.ppermute(gathered[2:], "space", swap)

    outgoing_shapes = (
        shape((chips, 2, latent)),
        shape((3 * HALO, latent)),
        shape((2 * HALO, latent)),
    )
    scratch = [
        pltpu.VMEM((4, latent, latent), BF),
        pltpu.VMEM((EXTRA, latent), BF),
        pltpu.VMEM((2 * ROWS + 8 * HALO + owners, latent), BF),
        pltpu.VMEM((table_rows, latent), BF),
        pltpu.SemaphoreType.DMA((5,)),
    ]
    coarse, halo, inner = call(prepare_kernel, outgoing_shapes, core, state, halo_hot, smem=1)
    for layer in range(4):
        coarse = lax.all_to_all(coarse, "space", 0, 0, tiled=True, axis_index_groups=same_core)
        coarse = coarse.reshape(owners, latent)
        halo = gather_pair(to_next(halo))
        inputs = (core, state, halo, inner, coarse, edges_hot, sums_hot)
        if layer < 2:
            state, coarse, halo, inner = call(
                functools.partial(early_layer_kernel, layer=layer),
                (shape(state.shape),) + outgoing_shapes,
                *inputs, halo_hot, process_weight[0], half, partner, partner_other,
                smem=1, hbm=4, scratch=scratch,
            )
        elif layer < 3:
            state, coarse, halo, inner = call(
                functools.partial(late_layer_kernel, layer=layer),
                (shape(state.shape),) + outgoing_shapes,
                *inputs, halo_hot, gathered, gathered_other,
                smem=1, hbm=2, scratch=scratch,
            )
        else:
            keys = call(
                functools.partial(last_layer_kernel, layer=layer),
                shape((sections, ROWS, latent)),
                *inputs, decode_weight[0], gathered, gathered_other,
                smem=1, hbm=2, scratch=scratch,
            )

    keys = lax.all_to_all(keys, "section", 0, 0, tiled=True)
    own, near, far = call(deliver_kernel, (block, block, block), core, keys, decode_senders[0], smem=1)
    far = to_next(far)
    near = gather_pair(near)
    return call(
        decode_kernel,
        shape((samples, grid_rows, output_weight.shape[1])),
        core, own, near, far, queries, decode_features[:, 0, 0, :], decode_edge_weight, vec(decode_bias),
        decode_receivers[0], x, output_weight,
        smem=1,
    )


def solution(mesh):
    return jax.shard_map(
        shards,
        mesh=mesh,
        in_specs=(
            P(None, ("section", "space"), None),
            P(),
            P(),
            P(),
            P(),
            P(),
            P(),
            P("section", None, None, None),
            P("section", None, None),
            P("section", None, None),
            P("section", None),
            P(),
            P(),
            P(),
            P(),
            P("section", "space", None),
            P("section", "space", None),
            P(None, "section", "space", None),
            P("space", None),
            P("space", None),
            P("space", None),
            P(None, "space", None),
            P("section", "space", None),
            P("section", "space", None),
            P(None, "section", "space", None),
        ),
        out_specs=P(None, ("section", "space"), None),
        check_vma=False,
    )
```

time: 582 us -> 300 us (0.52)
  the two profiles are of different devices: /device:TPU:25 before, /device:TPU:2 now
where the time goes in v1:
time: 300 us; the launch traced here: 298 us
  waiting for transfers between devices  107 us (36%)
  starting transfers between devices  90.1 us (30%)
  local copies, waits for them, and re-layouts  32.8 us (11%)
  blocking collectives  28.4 us (9%)
  Pallas kernels  25.5 us (8%)
  between operations  14 us (5%)
    all_gather x1, waiting for transfers between devices, shards(): gathered = lax.all_gather(sent_half, 'section', axis=0)  60 us
    ppermute x6, starting transfers between devices, to_next(): return lax.ppermute(value, 'space', to_neighbour)  38.7 us
    all_to_all x4, starting transfers between devices, shards(): lax.all_to_all(coarse, 'space', 0, 0, tiled=True, axis_index_groups=same_...  34.3 us
    pallas_call x12, Pallas kernels, call(): pl.pallas_call(kernel, out_shape=out, in_specs=specs, out_specs=jax.tree....  25.5 us
    unnamed x115, local copies, waits for them, and re-layouts  25 us
    ppermute x1, waiting for transfers between devices, shards(): lax.ppermute(half, 'section', [(i, i ^ 1) for i in range(sections)])  20.7 us
    all_gather x8, blocking collectives, gather_pair(): return lax.all_gather(value, 'space', axis=0, axis_index_groups=pairs)  16.2 us
    ppermute x6, waiting for transfers between devices, to_next(): return lax.ppermute(value, 'space', to_neighbour)  14 us
  transfers between devices with their start and end apart: 15, of which 12 were waited for; matrix products, arithmetic and copies ran while one was open for 1% of the time, Pallas kernels for 5%

profile of v1, /device:TPU:2, one launch (start us, length us, event | category | flops | bytes accessed | tf_op | source)
XLA Modules:
  0.0 298.1 jit_solution(12737464649612202293)
XLA Ops:
  11.8 7.8 %collective-permute-start.2 = (bf16[1088,512]{1,0:T(8,128)(2,1)}, bf16[1088,512]{1,0:T(8,128)(2,1)}, u32[]{:S(2)}, u32[]{:S(2)}) collective-permute-start(bf16[1088,512]{1,0:T(8,128)(2,1)} %shard_map.240.own_half), channel_id=1, source_target_pairs={{0,128},{128,0},{256,384},{384,256},{1,129},{129,1},{257,385},{385... | collective-permute-start | bytes 3342344 | tf_op jit(solution)/shard_map/ppermute | solution.py:397
  19.7 20.7 %collective-permute-done.2.mine = bf16[1088,512]{1,0:T(8,128)(2,1)} collective-permute-done((bf16[1088,512]{1,0:T(8,128)(2,1)}, bf16[1088,512]{1,0:T(8,128)(2,1)}, u32[]{:S(2)}, u32[]{:S(2)}) %collective-permute-start.2) | collective-permute-done | bytes 1114144 | tf_op jit(solution)/shard_map/ppermute | solution.py:397
  40.4 60.0 %all-gather.11.cloned.1.call-done = bf16[4352,512]{1,0:T(8,128)(2,1)} async-done(((bf16[1088,512]{1,0:T(8,128)(2,1)}), bf16[4352,512]{1,0:T(8,128)(2,1)}) %all-gather.11.cloned.1.call-update) | async-done | bytes 4456464 | tf_op jit(solution)/shard_map/all_gather | solution.py:442
  100.4 3.2 %slice.37 = bf16[2176,512]{1,0:T(8,128)(2,1)} slice(bf16[4352,512]{1,0:T(8,128)(2,1)} %all-gather.11.cloned.1.call-done), slice={[2176:4352], [0:512]} | slice | bytes 4456448 | tf_op jit(solution)/shard_map/slice | solution.py:443
  109.0 8.2 %collective-permute-start = (bf16[128,512]{1,0:T(8,128)(2,1)S(1)}, bf16[128,512]{1,0:T(8,128)(2,1)S(1)}, u32[]{:S(2)}, u32[]{:S(2)}) collective-permute-start(bf16[128,512]{1,0:T(8,128)(2,1)S(1)} %get-tuple-element.33), channel_id=1, source_target_pairs={{1,2},{3,4},{5,6},{7,8},{9,10},{11,12},{13,14},{15,16},{17,18},{19... | collective-permute-start | bytes 393224 | tf_op jit(solution)/shard_map/ppermute | solution.py:384
  124.1 5.3 %all-to-all-start = ((bf16[4,128,512]{2,1,0:T(8,128)(2,1)}), bf16[4,128,512]{2,1,0:T(8,128)(2,1)}, u32[]{:S(2)}, u32[]{:S(2)}) async-start(bf16[4,128,512]{2,1,0:T(8,128)(2,1)} %shard_map.236), calls=%async_computation | async-start | bytes 1048576 | tf_op jit(solution)/shard_map/all_to_all | solution.py:436
  132.6 5.5 %all-to-all-done.parts = bf16[4,128,512]{2,1,0:T(8,128)(2,1)} async-done(((bf16[4,128,512]{2,1,0:T(8,128)(2,1)}), bf16[4,128,512]{2,1,0:T(8,128)(2,1)}, u32[]{:S(2)}, u32[]{:S(2)}) %all-to-all-start) | async-done | bytes 524320 | tf_op jit(solution)/shard_map/all_to_all | solution.py:436
  144.8 7.9 %all-to-all-start.1 = ((bf16[64,2,512]{2,1,0:T(2,128)(2,1)}), bf16[64,2,512]{2,1,0:T(2,128)(2,1)}, u32[]{:S(2)}, u32[]{:S(2)}) async-start(bf16[64,2,512]{2,1,0:T(2,128)(2,1)} %copy-done.25), calls=%async_computation.1 | async-start | bytes 262144 | tf_op jit(solution)/shard_map/all_to_all | solution.py:459
  152.7 6.2 %collective-permute-start.1 = (bf16[48,512]{1,0:T(8,128)(2,1)}, bf16[48,512]{1,0:T(8,128)(2,1)S(1)}, u32[]{:S(2)}, u32[]{:S(2)}) collective-permute-start(bf16[48,512]{1,0:T(8,128)(2,1)} %copy-done.45), channel_id=1, source_target_pairs={{1,2},{3,4},{5,6},{7,8},{9,10},{11,12},{13,14},{15,16},{17,18},{19... | collective-permute-start | bytes 147464 | tf_op jit(solution)/shard_map/ppermute | solution.py:384
  159.0 3.0 %collective-permute-done.1 = bf16[48,512]{1,0:T(8,128)(2,1)S(1)} collective-permute-done((bf16[48,512]{1,0:T(8,128)(2,1)}, bf16[48,512]{1,0:T(8,128)(2,1)S(1)}, u32[]{:S(2)}, u32[]{:S(2)}) %collective-permute-start.1) | collective-permute-done | bytes 49184 | tf_op jit(solution)/shard_map/ppermute | solution.py:384
  170.5 4.4 %shard_map.241 = (bf16[256,512]{1,0:T(8,128)(2,1)S(1)}, bf16[64,2,512]{2,1,0:T(2,128)(2,1)S(1)}, bf16[48,512]{1,0:T(8,128)(2,1)S(1)}, bf16[32,512]{1,0:T(8,128)(2,1)S(1)}) custom-call(s32[2]{0:T(128)S(1)} %pad_add_fusion.core, bf16[256,512]{1,0:T(8,128)(2,1)S(1)} %all-gather.1.state, bf16[2,48,512]{2,1,0:T(8,128)(2,1)S(1)} %bitcast.64, ...), custom_call_target="tpu_custom_call" | custom-call | flops 1000000 | bytes 1000000 | tf_op jit(solution)/shard_map/pallas_call | solution.py:75
  177.4 9.0 %all-to-all-start.2 = ((bf16[64,2,512]{2,1,0:T(2,128)(2,1)}), bf16[64,2,512]{2,1,0:T(2,128)(2,1)}, u32[]{:S(2)}, u32[]{:S(2)}) async-start(bf16[64,2,512]{2,1,0:T(2,128)(2,1)} %copy-done.24), calls=%async_computation.2 | async-start | bytes 262144 | tf_op jit(solution)/shard_map/all_to_all | solution.py:459
  186.4 6.2 %collective-permute-start.4 = (bf16[48,512]{1,0:T(8,128)(2,1)}, bf16[48,512]{1,0:T(8,128)(2,1)S(1)}, u32[]{:S(2)}, u32[]{:S(2)}) collective-permute-start(bf16[48,512]{1,0:T(8,128)(2,1)} %copy-done.44), channel_id=1, source_target_pairs={{1,2},{3,4},{5,6},{7,8},{9,10},{11,12},{13,14},{15,16},{17,18},{19... | collective-permute-start | bytes 147464 | tf_op jit(solution)/shard_map/ppermute | solution.py:384
  192.7 3.0 %collective-permute-done.4 = bf16[48,512]{1,0:T(8,128)(2,1)S(1)} collective-permute-done((bf16[48,512]{1,0:T(8,128)(2,1)}, bf16[48,512]{1,0:T(8,128)(2,1)S(1)}, u32[]{:S(2)}, u32[]{:S(2)}) %collective-permute-start.4) | collective-permute-done | bytes 49184 | tf_op jit(solution)/shard_map/ppermute | solution.py:384
  203.4 3.6 %shard_map.242 = (bf16[256,512]{1,0:T(8,128)(2,1)S(1)}, bf16[64,2,512]{2,1,0:T(2,128)(2,1)S(1)}, bf16[48,512]{1,0:T(8,128)(2,1)S(1)}, bf16[32,512]{1,0:T(8,128)(2,1)S(1)}) custom-call(s32[2]{0:T(128)S(1)} %pad_add_fusion.core, bf16[256,512]{1,0:T(8,128)(2,1)S(1)} %copy-done.18, bf16[2,48,512]{2,1,0:T(8,128)(2,1)S(1)} %bitcast.65, ...), custom_call_target="tpu_custom_call" | custom-call | flops 1000000 | bytes 1000000 | tf_op jit(solution)/shard_map/pallas_call | solution.py:75
  209.0 8.9 %all-to-all-start.3 = ((bf16[64,2,512]{2,1,0:T(2,128)(2,1)}), bf16[64,2,512]{2,1,0:T(2,128)(2,1)S(1)}, u32[]{:S(2)}, u32[]{:S(2)}) async-start(bf16[64,2,512]{2,1,0:T(2,128)(2,1)} %copy-done.23), calls=%async_computation.3 | async-start | bytes 262144 | tf_op jit(solution)/shard_map/all_to_all | solution.py:459
  217.9 6.3 %collective-permute-start.5 = (bf16[48,512]{1,0:T(8,128)(2,1)}, bf16[48,512]{1,0:T(8,128)(2,1)S(1)}, u32[]{:S(2)}, u32[]{:S(2)}) collective-permute-start(bf16[48,512]{1,0:T(8,128)(2,1)} %copy-done.43), channel_id=1, source_target_pairs={{1,2},{3,4},{5,6},{7,8},{9,10},{11,12},{13,14},{15,16},{17,18},{19... | collective-permute-start | bytes 147464 | tf_op jit(solution)/shard_map/ppermute | solution.py:384
  224.2 2.9 collective-permute-done.5
  234.1 4.2 %shard_map.243 = (bf16[256,512]{1,0:T(8,128)(2,1)S(1)}, bf16[64,2,512]{2,1,0:T(2,128)(2,1)}, bf16[48,512]{1,0:T(8,128)(2,1)S(1)}, bf16[32,512]{1,0:T(8,128)(2,1)S(1)}) custom-call(s32[2]{0:T(128)S(1)} %pad_add_fusion.core, bf16[256,512]{1,0:T(8,128)(2,1)S(1)} %copy-done.20, bf16[2,48,512]{2,1,0:T(8,128)(2,1)S(1)} %bitcast.63, ...), custom_call_target="tpu_custom_call" | custom-call | flops 1000000 | bytes 1000000 | tf_op jit(solution)/shard_map/pallas_call | solution.py:75
  238.3 8.5 %all-to-all-start.4 = ((bf16[64,2,512]{2,1,0:T(2,128)(2,1)}), bf16[64,2,512]{2,1,0:T(2,128)(2,1)S(1)}, u32[]{:S(2)}, u32[]{:S(2)}) async-start(bf16[64,2,512]{2,1,0:T(2,128)(2,1)} %get-tuple-element.52), calls=%async_computation.4 | async-start | bytes 262144 | tf_op jit(solution)/shard_map/all_to_all | solution.py:459
  246.8 7.0 %collective-permute-start.7 = (bf16[48,512]{1,0:T(8,128)(2,1)S(1)}, bf16[48,512]{1,0:T(8,128)(2,1)S(1)}, u32[]{:S(2)}, u32[]{:S(2)}) collective-permute-start(bf16[48,512]{1,0:T(8,128)(2,1)S(1)} %get-tuple-element.50), channel_id=1, source_target_pairs={{1,2},{3,4},{5,6},{7,8},{9,10},{11,12},{13,14},{15,16},{17,18},{19... | collective-permute-start | bytes 147464 | tf_op jit(solution)/shard_map/ppermute | solution.py:384
  262.7 3.5 %shard_map.244 = bf16[4,128,512]{2,1,0:T(8,128)(2,1)S(1)} custom-call(s32[2]{0:T(128)S(1)} %pad_add_fusion.core, bf16[256,512]{1,0:T(8,128)(2,1)S(1)} %get-tuple-element.49.state, bf16[2,48,512]{2,1,0:T(8,128)(2,1)S(1)} %bitcast.66, bf16[32,512]{1,0:T(8,128)(2,1)S(1)} %get-tuple-element.51.inner, bf16[128,512]{1,0:T(8,128)(2,1)S(1)} %reshape.47.coarse, ...), custom_call_target="tpu_custom_call" | custom-call | flops 1000000 | bytes 1000000 | tf_op jit(solution)/shard_map/pallas_call | solution.py:75
  266.3 12.2 %all_to_all.30.keys = bf16[4,128,512]{2,1,0:T(8,128)(2,1)S(1)} all-to-all(bf16[4,128,512]{2,1,0:T(8,128)(2,1)S(1)} %shard_map.244), channel_id=1, replica_groups=mesh['section'=4,'space'=128] {'section'}, dimensions={0} | all-to-all | bytes 1048576 | tf_op jit(solution)/shard_map/all_to_all | solution.py:485
  279.4 4.7 %collective-permute-start.8 = (bf16[128,512]{1,0:T(8,128)(2,1)S(1)}, bf16[128,512]{1,0:T(8,128)(2,1)S(1)}, u32[]{:S(2)}, u32[]{:S(2)}) collective-permute-start(bf16[128,512]{1,0:T(8,128)(2,1)S(1)} %get-tuple-element.55), channel_id=1, source_target_pairs={{1,2},{3,4},{5,6},{7,8},{9,10},{11,12},{13,14},{15,16},{17,18},{19... | collective-permute-start | bytes 393224 | tf_op jit(solution)/shard_map/ppermute | solution.py:384
  (162 shorter events, 71.9 us)
Async XLA Ops:
  6.5 93.8 %all-gather.11.cloned.1.call-start = ((), (), s32[]{:S(2)}) async-start(), calls=%async_computation.6 | async-start | bytes 5570560 | tf_op jit(solution)/shard_map/all_gather | solution.py:442
  11.8 28.5 %collective-permute-start.2 = (bf16[1088,512]{1,0:T(8,128)(2,1)}, bf16[1088,512]{1,0:T(8,128)(2,1)}, u32[]{:S(2)}, u32[]{:S(2)}) collective-permute-start(bf16[1088,512]{1,0:T(8,128)(2,1)} %shard_map.240.own_half), channel_id=1, source_target_pairs={{0,128},{128,0},{256,384},{384,256},{1,129},{129,1},{257,385},{385... | collective-permute-start | bytes 3342344 | tf_op jit(solution)/shard_map/ppermute | solution.py:397
  40.4 65.3 %copy-start.47 = (bf16[2,128,474]{1,0,2:T(2,128)(2,1)S(1)}, bf16[2,128,474]{1,0,2:T(2,128)(2,1)}, u32[]{:S(2)}) copy-start(bf16[2,128,474]{1,0,2:T(2,128)(2,1)} %param.25) | copy-start | bytes 728068
  40.4 65.5 %copy-start.46 = (bf16[2,512,512]{2,1,0:T(8,128)(2,1)S(1)}, bf16[2,512,512]{2,1,0:T(8,128)(2,1)}, u32[]{:S(2)}) copy-start(bf16[2,512,512]{2,1,0:T(8,128)(2,1)} %param.36) | copy-start | bytes 3145732
  103.6 127.2 %collective-permute-start.6 = (bf16[2,1088,512]{2,1,0:T(8,128)(2,1)}, bf16[2,1088,512]{2,1,0:T(8,128)(2,1)}, u32[]{:S(2)}, u32[]{:S(2)}) collective-permute-start(bf16[2,1088,512]{2,1,0:T(8,128)(2,1)} %bitcast.23), channel_id=1, source_target_pairs={{0,1},{1,0},{2,3},{3,2},{4,5},{5,4},{6,7},{7,6},{8,9},{9,8},{10,11... | collective-permute-start | bytes 6684680 | tf_op jit(solution)/shard_map/ppermute | solution.py:443
  106.8 22.7 %copy-start.50 = (f32[4,1,448]{2,1,0:T(1,128)S(1)}, f32[4,1,448]{2,1,0:T(1,128)}, u32[]{:S(2)}) copy-start(f32[4,1,448]{2,1,0:T(1,128)} %param.46) | copy-start | bytes 21508
  106.8 31.3 %copy-start.37 = (f32[512]{0:T(512)S(1)}, f32[512]{0:T(512)}, u32[]{:S(2)}) copy-start(f32[512]{0:T(512)} %param.31) | copy-start | bytes 6148
  109.0 13.1 %collective-permute-start = (bf16[128,512]{1,0:T(8,128)(2,1)S(1)}, bf16[128,512]{1,0:T(8,128)(2,1)S(1)}, u32[]{:S(2)}, u32[]{:S(2)}) collective-permute-start(bf16[128,512]{1,0:T(8,128)(2,1)S(1)} %get-tuple-element.33), channel_id=1, source_target_pairs={{1,2},{3,4},{5,6},{7,8},{9,10},{11,12},{13,14},{15,16},{17,18},{19... | collective-permute-start | bytes 393224 | tf_op jit(solution)/shard_map/ppermute | solution.py:384
  117.3 49.8 %collective-permute-start.3 = (bf16[1088,512]{1,0:T(8,128)(2,1)}, bf16[1088,512]{1,0:T(8,128)(2,1)}, u32[]{:S(2)}, u32[]{:S(2)}) collective-permute-start(bf16[1088,512]{1,0:T(8,128)(2,1)} %collective-permute-done.2.mine), channel_id=1, source_target_pairs={{0,1},{1,0},{2,3},{3,2},{4,5},{5,4},{6,7},{7,6},{8,9},{9,8},{10,11... | collective-permute-start | bytes 3342344 | tf_op jit(solution)/shard_map/ppermute | solution.py:440
  122.2 44.9 %copy-start.3 = (bf16[1,4,512,512]{3,2,1,0:T(8,128)(2,1)S(1)}, bf16[1,4,512,512]{3,2,1,0:T(8,128)(2,1)}, u32[]{:S(2)}) copy-start(bf16[1,4,512,512]{3,2,1,0:T(8,128)(2,1)} %param.32) | copy-start | bytes 6291460
  124.1 14.0 %all-to-all-start = ((bf16[4,128,512]{2,1,0:T(8,128)(2,1)}), bf16[4,128,512]{2,1,0:T(8,128)(2,1)}, u32[]{:S(2)}, u32[]{:S(2)}) async-start(bf16[4,128,512]{2,1,0:T(8,128)(2,1)} %shard_map.236), calls=%async_computation | async-start | bytes 1048576 | tf_op jit(solution)/shard_map/all_to_all | solution.py:436
  144.8 20.6 %all-to-all-start.1 = ((bf16[64,2,512]{2,1,0:T(2,128)(2,1)}), bf16[64,2,512]{2,1,0:T(2,128)(2,1)}, u32[]{:S(2)}, u32[]{:S(2)}) async-start(bf16[64,2,512]{2,1,0:T(2,128)(2,1)} %copy-done.25), calls=%async_computation.1 | async-start | bytes 262144 | tf_op jit(solution)/shard_map/all_to_all | solution.py:459
  152.7 9.2 %collective-permute-start.1 = (bf16[48,512]{1,0:T(8,128)(2,1)}, bf16[48,512]{1,0:T(8,128)(2,1)S(1)}, u32[]{:S(2)}, u32[]{:S(2)}) collective-permute-start(bf16[48,512]{1,0:T(8,128)(2,1)} %copy-done.45), channel_id=1, source_target_pairs={{1,2},{3,4},{5,6},{7,8},{9,10},{11,12},{13,14},{15,16},{17,18},{19... | collective-permute-start | bytes 147464 | tf_op jit(solution)/shard_map/ppermute | solution.py:384
  177.4 21.6 %all-to-all-start.2 = ((bf16[64,2,512]{2,1,0:T(2,128)(2,1)}), bf16[64,2,512]{2,1,0:T(2,128)(2,1)}, u32[]{:S(2)}, u32[]{:S(2)}) async-start(bf16[64,2,512]{2,1,0:T(2,128)(2,1)} %copy-done.24), calls=%async_computation.2 | async-start | bytes 262144 | tf_op jit(solution)/shard_map/all_to_all | solution.py:459
  186.4 9.3 %collective-permute-start.4 = (bf16[48,512]{1,0:T(8,128)(2,1)}, bf16[48,512]{1,0:T(8,128)(2,1)S(1)}, u32[]{:S(2)}, u32[]{:S(2)}) collective-permute-start(bf16[48,512]{1,0:T(8,128)(2,1)} %copy-done.44), channel_id=1, source_target_pairs={{1,2},{3,4},{5,6},{7,8},{9,10},{11,12},{13,14},{15,16},{17,18},{19... | collective-permute-start | bytes 147464 | tf_op jit(solution)/shard_map/ppermute | solution.py:384
  203.4 27.4 %copy-start.11 = (bf16[128,256]{1,0:T(8,128)(2,1)S(1)}, bf16[128,256]{1,0:T(8,128)(2,1)}, u32[]{:S(2)}) copy-start(bf16[128,256]{1,0:T(8,128)(2,1)} %copy-done.7) | copy-start | bytes 196612
  209.0 21.8 %all-to-all-start.3 = ((bf16[64,2,512]{2,1,0:T(2,128)(2,1)}), bf16[64,2,512]{2,1,0:T(2,128)(2,1)S(1)}, u32[]{:S(2)}, u32[]{:S(2)}) async-start(bf16[64,2,512]{2,1,0:T(2,128)(2,1)} %copy-done.23), calls=%async_computation.3 | async-start | bytes 262144 | tf_op jit(solution)/shard_map/all_to_all | solution.py:459
  217.9 9.2 %collective-permute-start.5 = (bf16[48,512]{1,0:T(8,128)(2,1)}, bf16[48,512]{1,0:T(8,128)(2,1)S(1)}, u32[]{:S(2)}, u32[]{:S(2)}) collective-permute-start(bf16[48,512]{1,0:T(8,128)(2,1)} %copy-done.43), channel_id=1, source_target_pairs={{1,2},{3,4},{5,6},{7,8},{9,10},{11,12},{13,14},{15,16},{17,18},{19... | collective-permute-start | bytes 147464 | tf_op jit(solution)/shard_map/ppermute | solution.py:384
  234.1 26.4 %copy-start.6 = (bf16[512,512]{1,0:T(8,128)(2,1)S(1)}, bf16[512,512]{1,0:T(8,128)(2,1)}, u32[]{:S(2)}) copy-start(bf16[512,512]{1,0:T(8,128)(2,1)} %get-tuple-element.57.decode) | copy-start | bytes 1572868
  238.3 22.1 %all-to-all-start.4 = ((bf16[64,2,512]{2,1,0:T(2,128)(2,1)}), bf16[64,2,512]{2,1,0:T(2,128)(2,1)S(1)}, u32[]{:S(2)}, u32[]{:S(2)}) async-start(bf16[64,2,512]{2,1,0:T(2,128)(2,1)} %get-tuple-element.52), calls=%async_computation.4 | async-start | bytes 262144 | tf_op jit(solution)/shard_map/all_to_all | solution.py:459
  246.8 9.4 %collective-permute-start.7 = (bf16[48,512]{1,0:T(8,128)(2,1)S(1)}, bf16[48,512]{1,0:T(8,128)(2,1)S(1)}, u32[]{:S(2)}, u32[]{:S(2)}) collective-permute-start(bf16[48,512]{1,0:T(8,128)(2,1)S(1)} %get-tuple-element.50), channel_id=1, source_target_pairs={{1,2},{3,4},{5,6},{7,8},{9,10},{11,12},{13,14},{15,16},{17,18},{19... | collective-permute-start | bytes 147464 | tf_op jit(solution)/shard_map/ppermute | solution.py:384
  266.3 22.7 %copy-start.5 = (bf16[2,128,474]{2,1,0:T(8,128)(2,1)S(1)}, bf16[2,128,474]{2,1,0:T(8,128)(2,1)}, u32[]{:S(2)}) copy-start(bf16[2,128,474]{2,1,0:T(8,128)(2,1)} %copy-done.4) | copy-start | bytes 728068
  266.3 22.7 %copy-start.22 = (bf16[256,512]{1,0:T(8,128)(2,1)S(1)}, bf16[256,512]{1,0:T(8,128)(2,1)}, u32[]{:S(2)}) copy-start(bf16[256,512]{1,0:T(8,128)(2,1)} %copy-done.21) | copy-start | bytes 786436
  279.4 9.6 %collective-permute-start.8 = (bf16[128,512]{1,0:T(8,128)(2,1)S(1)}, bf16[128,512]{1,0:T(8,128)(2,1)S(1)}, u32[]{:S(2)}, u32[]{:S(2)}) collective-permute-start(bf16[128,512]{1,0:T(8,128)(2,1)S(1)} %get-tuple-element.55), channel_id=1, source_target_pairs={{1,2},{3,4},{5,6},{7,8},{9,10},{11,12},{13,14},{15,16},{17,18},{19... | collective-permute-start | bytes 393224 | tf_op jit(solution)/shard_map/ppermute | solution.py:384
  (46 other events, 303.9 us)
Sparse Core Ops, SparseCore 0:
  40.5 59.8 all-gather.10

commit v2 on v1

--- a/solution.py
+++ b/solution.py
@@ -13,7 +13,8 @@
 HALO = 16
 EXTRA = 64
 NODE_BIAS, GAIN = 32, 35
-VMEM_LIMIT = 24 * 1024 * 1024
+SMALL_LIMIT = 16 * 1024 * 1024
+LAYER_LIMIT = 63_000_000
 
 
 def silu(v):
@@ -61,25 +62,25 @@
     return dot_t(feature_parts(features).astype(BF), weight_parts(weight).astype(BF))
 
 
-def call(kernel, out, *args, smem=0, hbm=0, scratch=(), hbm_out=False, cost=1_000_000):
+def call(kernel, out, *args, smem=0, hbm=0, scratch=(), hbm_out=False, limit=SMALL_LIMIT):
     count = len(args)
     specs = []
     for position in range(count):
         if position < smem:
             specs.append(pl.BlockSpec(memory_space=pltpu.SMEM))
         elif position >= count - hbm:
-            specs.append(pl.BlockSpec(memory_space=pl.ANY))
+            specs.append(pl.BlockSpec(memory_space=pltpu.HBM))
         else:
             specs.append(pl.BlockSpec(memory_space=pltpu.VMEM))
-    out_spec = pl.BlockSpec(memory_space=pl.ANY if hbm_out else pltpu.VMEM)
+    out_spec = pl.BlockSpec(memory_space=pltpu.HBM if hbm_out else pltpu.VMEM)
     return pl.pallas_call(
         kernel,
         out_shape=out,
         in_specs=specs,
         out_specs=jax.tree.map(lambda _: out_spec, out),
         scratch_shapes=list(scratch),
-        compiler_params=pltpu.CompilerParams(vmem_limit_bytes=VMEM_LIMIT),
-        cost_estimate=pl.CostEstimate(flops=cost, bytes_accessed=1_000_000, transcendentals=0),
+        compiler_params=pltpu.CompilerParams(vmem_limit_bytes=limit),
+        cost_estimate=pl.CostEstimate(flops=1_000_000, bytes_accessed=1_000_000, transcendentals=0),
     )(*args)
 
 
@@ -87,18 +88,25 @@
     return jax.ShapeDtypeStruct(dims, dtype)
 
 
-def pack_weights_kernel(core, edge_weight, bias, gain, weight, out, extras, sems):
-    half = 2 * weight.shape[1]
-    first = [
+def pack_weights_kernel(core, edge_from, bias_from, gain_from, weight, out, edge_weight, bias, gain, packed, sems):
+    size = weight.shape[1]
+    half = 2 * size
+    vectors = [
+        pltpu.make_async_copy(source, target, sems.at[2 + i])
+        for i, (source, target) in enumerate(
+            ((edge_from, edge_weight), (bias_from, bias), (gain_from, gain))
+        )
+    ]
+    matrices = [
         pltpu.make_async_copy(
-            weight.at[2 * core[0] + m],
-            out.at[pl.ds(m * (half // 2), half // 2)],
-            sems.at[m],
+            weight.at[2 * core[0] + m], packed.at[pl.ds(m * size, size)], sems.at[m]
         )
         for m in range(2)
     ]
-    for copy in first:
+    for copy in vectors + matrices:
         copy.start()
+    for copy in vectors:
+        copy.wait()
     width = edge_weight.shape[1]
     b_parts = [p.astype(F32) for p in split3(bias[0:1, :])]
     n_parts = [p.astype(F32) for p in split3(bias[1:2, :])]
@@ -112,12 +120,12 @@
         + [jnp.zeros((EXTRA - 38, width), F32)],
         axis=0,
     )
-    extras[...] = rows.astype(BF)
-    tail = pltpu.make_async_copy(extras, out.at[pl.ds(half, EXTRA)], sems.at[2])
-    tail.start()
-    for copy in first:
+    packed[half:] = rows.astype(BF)
+    for copy in matrices:
         copy.wait()
-    tail.wait()
+    whole = pltpu.make_async_copy(packed, out, sems.at[0])
+    whole.start()
+    whole.wait()
 
 
 def setup_kernel(meta, edges_out, sums_out, halo_out, *, coarse):
@@ -159,7 +167,7 @@
     latent = silu(dot(x[...], embed_weight[...]) + embed_bias[...]).astype(BF)
     keys = dot(latent, encode_weight[...]).astype(BF)
     send_blocks(core, keys, senders, own, near, far)
-    queries[...] = dot(latent, query_weight[...]).astype(BF)
+    queries[...] = dot(latent, query_weight[1]).astype(BF)
 
 
 def send_blocks(core, keys, senders, own, near, far):
@@ -179,7 +187,7 @@
     cap = own.shape[0] // 2
     at = pl.ds(sample * cap, cap)
     from_near = jnp.where(first, near[1, at], near[0, at])
-    from_far = far[at]
+    from_far = jnp.where(first, far[0, at], far[1, at])
     return jnp.concatenate(
         [own[at], jnp.where(first, from_far, from_near), jnp.where(first, from_near, from_far)],
         axis=0,
@@ -216,20 +224,79 @@
     outgoing(core, state[...], halo_hot, coarse_out, halo_out, inner_out)
 
 
-def layer_body(state, halo, inner, coarse, edges_hot, sums_hot, wbuf, ebuf, sources, table, waits):
-    coarse_rows = coarse.shape[0]
+def fetch_weights(core, wbuf, ebuf, sems, mine, other):
+    size = wbuf.shape[1]
+
+    def start(m):
+        at = pl.ds((m % 2) * size, size)
+
+        @pl.when(core[0] == m // 2)
+        def _():
+            pltpu.make_async_copy(mine.at[at], wbuf.at[m], sems.at[m]).start()
+
+        @pl.when(core[0] != m // 2)
+        def _():
+            pltpu.make_async_copy(other.at[at], wbuf.at[m], sems.at[m]).start()
+
+        return pltpu.make_async_copy(mine.at[at], wbuf.at[m], sems.at[m])
+
+    tail = pltpu.make_async_copy(mine.at[pl.ds(2 * size, EXTRA)], ebuf, sems.at[4])
+    return start, tail
+
+
+def layer_kernel(core, *refs, layer, last):
+    refs = list(refs)
+
+    def take(count):
+        taken = refs[:count]
+        del refs[:count]
+        return taken
+
+    state, halo, inner, coarse, edges_hot, sums_hot, tail_from = take(7)
+    mine, other = take(2)
+    outs = take(1 if last else 4)
+    wbuf, ebuf, sources, table, hot, sums, tail_weight, sems = take(8)
+    staged = take(len(outs))
+    (out_sems,) = refs
+
     at_halo = 2 * ROWS
     at_inner = at_halo + 6 * HALO
     at_coarse = at_inner + 2 * HALO
-    sources[0:at_halo] = state[...]
-    sources[at_halo : at_halo + 3 * HALO] = halo[0]
-    sources[at_halo + 3 * HALO : at_inner] = halo[1]
-    sources[at_inner:at_coarse] = inner[...]
-    sources[at_coarse : at_coarse + coarse_rows] = coarse[...]
+    coarse_rows = coarse.shape[0]
+    in_place = [
+        pltpu.make_async_copy(source, sources.at[pl.ds(at, count)], sems.at[5 + i])
+        for i, (source, at, count) in enumerate(
+            (
+                (state, 0, 2 * ROWS),
+                (halo.at[0, 0], at_halo, 3 * HALO),
+                (halo.at[1, 1], at_halo + 3 * HALO, 3 * HALO),
+                (inner, at_inner, 2 * HALO),
+                (coarse, at_coarse, coarse_rows),
+            )
+        )
+    ]
+    for copy in in_place:
+        copy.start()
+    later = [
+        pltpu.make_async_copy(edges_hot, hot, sems.at[10]),
+        pltpu.make_async_copy(sums_hot, sums, sems.at[11]),
+        pltpu.make_async_copy(tail_from.at[0] if last else tail_from, tail_weight, sems.at[12]),
+    ]
+    start, vectors = fetch_weights(core, wbuf, ebuf, sems, mine.at[layer], other.at[layer])
+    waits = [start(0), start(1)]
+    vectors.start()
+    later[0].start()
+    later[1].start()
+    waits += [start(2), start(3), vectors]
+    later[2].start()
+
+    for copy in in_place:
+        copy.wait()
     waits[0].wait()
     keys = dot(sources[...], wbuf[0]).astype(BF)
     waits[1].wait()
-    target = dot(state[...], wbuf[1]).astype(BF)
+    old = sources[0:at_halo]
+    target = dot(old, wbuf[1]).astype(BF)
     up, down = at_halo, at_halo + 3 * HALO
     halo_from = (
         (up + HALO, at_inner, up, down + HALO),
@@ -237,105 +304,44 @@
     )
     at_target = ROWS + 4 * HALO + coarse_rows
     waits[4].wait()
+    later[0].wait()
+    later[1].wait()
     nodes = []
     for owner in range(2):
-        table[0:ROWS] = keys[owner * ROWS : (owner + 1) * ROWS]
+        table[owner, 0:ROWS] = keys[owner * ROWS : (owner + 1) * ROWS]
         for block in range(4):
             source = halo_from[owner][block]
-            table[ROWS + block * HALO : ROWS + (block + 1) * HALO] = keys[source : source + HALO]
-        table[ROWS + 4 * HALO : at_target] = keys[at_coarse : at_coarse + coarse_rows]
-        table[at_target : at_target + ROWS] = target[owner * ROWS : (owner + 1) * ROWS]
-        table[at_target + ROWS :] = ebuf[...]
-        hidden = silu(dot(edges_hot[owner], table[...])).astype(BF)
-        nodes.append(dot(sums_hot[owner], hidden).astype(BF))
+            table[owner, ROWS + block * HALO : ROWS + (block + 1) * HALO] = keys[source : source + HALO]
+        table[owner, ROWS + 4 * HALO : at_target] = keys[at_coarse : at_coarse + coarse_rows]
+        table[owner, at_target : at_target + ROWS] = target[owner * ROWS : (owner + 1) * ROWS]
+        table[owner, at_target + ROWS :] = ebuf[...]
+        hidden = silu(dot(hot[owner], table[owner])).astype(BF)
+        nodes.append(dot(sums[owner], hidden).astype(BF))
     node_in = jnp.concatenate(nodes, axis=0)
+    waits[3].wait()
+    kept = dot(old, wbuf[3])
     waits[2].wait()
-    waits[3].wait()
 
     def vector(at):
         return (ebuf[at : at + 1].astype(F32) + ebuf[at + 1 : at + 2].astype(F32)) + ebuf[
             at + 2 : at + 3
         ].astype(F32)
 
-    update = silu(dot(node_in, wbuf[2]) + dot(state[...], wbuf[3]) + vector(NODE_BIAS))
-    return (state[...].astype(F32) + layer_norm(update, vector(GAIN))).astype(BF)
-
-
-def fetch(core, wbuf, ebuf, sems, mine, other, use_own=None, own=None, own_half=None):
-    size = wbuf.shape[1]
-
-    def from_half(half, m):
-        return half.at[pl.ds((m % 2) * size, size)]
-
-    got = None if use_own is None else jnp.logical_not(use_own)
-
-    def both(condition):
-        return condition if got is None else jnp.logical_and(got, condition)
-
-    waits = []
-    for m in range(4):
-        if use_own is not None:
-
-            @pl.when(use_own)
-            def _(m=m):
-                pltpu.make_async_copy(own.at[m], wbuf.at[m], sems.at[m]).start()
-
-        @pl.when(both(core[0] == m // 2))
-        def _(m=m):
-            pltpu.make_async_copy(from_half(mine, m), wbuf.at[m], sems.at[m]).start()
-
-        @pl.when(both(core[0] != m // 2))
-        def _(m=m):
-            pltpu.make_async_copy(from_half(other, m), wbuf.at[m], sems.at[m]).start()
-
-        waits.append(pltpu.make_async_copy(from_half(mine, m), wbuf.at[m], sems.at[m]))
-    tail = pl.ds(2 * size, EXTRA)
-    if use_own is not None:
-
-        @pl.when(use_own)
-        def _():
-            pltpu.make_async_copy(own_half.at[tail], ebuf, sems.at[4]).start()
-
-        @pl.when(got)
-        def _():
-            pltpu.make_async_copy(mine.at[tail], ebuf, sems.at[4]).start()
-
+    update = silu(dot(node_in, wbuf[2]) + kept + vector(NODE_BIAS))
+    new = (old.astype(F32) + layer_norm(update, vector(GAIN))).astype(BF)
+    later[2].wait()
+    if last:
+        rows = jnp.where(core[0] == 0, new[:ROWS], new[ROWS:])
+        projected = dot(rows, tail_weight[...]).astype(BF)
+        staged[0][...] = projected
     else:
-        pltpu.make_async_copy(mine.at[tail], ebuf, sems.at[4]).start()
-    waits.append(pltpu.make_async_copy(mine.at[tail], ebuf, sems.at[4]))
-    return waits
-
-
-def early_layer_kernel(
-    core, state, halo, inner, coarse, edges_hot, sums_hot, halo_hot, own, own_half, mine, other,
-    state_out, coarse_out, halo_out, inner_out, wbuf, ebuf, sources, table, sems, *, layer,
-):
-    waits = fetch(core, wbuf, ebuf, sems, mine, other, core[1] == layer, own, own_half)
-    new = layer_body(state, halo, inner, coarse, edges_hot, sums_hot, wbuf, ebuf, sources, table, waits)
-    state_out[...] = new
-    outgoing(core, new, halo_hot, coarse_out, halo_out, inner_out)
-
-
-def late_layer_kernel(
-    core, state, halo, inner, coarse, edges_hot, sums_hot, halo_hot, mine, other,
-    state_out, coarse_out, halo_out, inner_out, wbuf, ebuf, sources, table, sems, *, layer,
-):
-    waits = fetch(core, wbuf, ebuf, sems, mine.at[layer], other.at[layer - 2])
-    new = layer_body(state, halo, inner, coarse, edges_hot, sums_hot, wbuf, ebuf, sources, table, waits)
-    state_out[...] = new
-    outgoing(core, new, halo_hot, coarse_out, halo_out, inner_out)
-
-
-def last_layer_kernel(
-    core, state, halo, inner, coarse, edges_hot, sums_hot, decode, mine, other,
-    keys_out, wbuf, ebuf, sources, table, sems, *, layer,
-):
-    waits = fetch(core, wbuf, ebuf, sems, mine.at[layer], other.at[layer - 2])
-    new = layer_body(state, halo, inner, coarse, edges_hot, sums_hot, wbuf, ebuf, sources, table, waits)
-    own = jnp.where(core[0] == 0, new[:ROWS], new[ROWS:])
-    keys = dot(own, decode[...]).astype(BF)
-    for section in range(keys_out.shape[0]):
-        keys_out[section] = keys
+        staged[0][...] = new
+        outgoing(core, new, tail_weight, *staged[1:])
+    sent = [pltpu.make_async_copy(a, b, out_sems.at[i]) for i, (a, b) in enumerate(zip(staged, outs))]
+    for copy in sent:
+        copy.start()
+    for copy in sent:
+        copy.wait()
 
 
 def deliver_kernel(core, keys, senders, own, near, far):
@@ -372,16 +378,14 @@
     core = jnp.stack([core_id, section % 2]).astype(jnp.int32)
     pairs = [[2 * k, 2 * k + 1] for k in range(chips)]
     same_core = [[2 * k + c for k in range(chips)] for c in range(2)]
-    to_neighbour = [(2 * k + 1, (2 * k + 2) % owners) for k in range(chips)] + [
-        (2 * k, (2 * k - 1) % owners) for k in range(chips)
-    ]
+    crossings = [[2 * k + 1, (2 * k + 2) % owners] for k in range(chips)]
     swap = [(i, i ^ 1) for i in range(owners)]
 
     def gather_pair(value):
         return lax.all_gather(value, "space", axis=0, axis_index_groups=pairs)
 
-    def to_next(value):
-        return lax.ppermute(value, "space", to_neighbour)
+    def gather_crossing(value):
+        return lax.all_gather(value, "space", axis=0, axis_index_groups=crossings)
 
     def vec(value):
         return value.reshape(1, -1)
@@ -391,21 +395,28 @@
         pack_weights_kernel,
         shape((half_rows, latent)),
         core, process_edge_weight[0], process_bias[0], process_gain, process_weight[0],
-        smem=1, hbm=1, hbm_out=True,
-        scratch=[pltpu.VMEM((EXTRA, latent), BF), pltpu.SemaphoreType.DMA((3,))],
-    )
-    partner = lax.ppermute(half, "section", [(i, i ^ 1) for i in range(sections)])
-
+        smem=1, hbm=4, hbm_out=True,
+        scratch=[
+            pltpu.VMEM(process_edge_weight.shape[1:], F32),
+            pltpu.VMEM(process_bias.shape[1:], F32),
+            pltpu.VMEM(process_gain.shape, F32),
+            pltpu.VMEM((half_rows, latent), BF),
+            pltpu.SemaphoreType.DMA((5,)),
+        ],
+    )
+    gathered = lax.all_gather(half, "section", axis=0)
+
+    grid_inputs, half = lax.optimization_barrier((grid_inputs, half))
     x = grid_inputs.reshape(samples * grid_rows, in_width)
     cap = encode_senders.shape[2] // 3
     block = shape((samples * cap, latent))
     own, near, far, queries = call(
         embed_kernel,
         (block, block, block, shape((samples * grid_rows, latent))),
-        core, x, embed_weight, vec(embed_bias), encode_weight, decode_weight[1], encode_senders[0],
+        core, x, embed_weight, vec(embed_bias), encode_weight, decode_weight, encode_senders[0],
         smem=1,
     )
-    far = to_next(far)
+    far = gather_crossing(far)
     near = gather_pair(near)
     edges = mesh_senders.shape[1]
     b = halo_send_rows.reshape(4, HALO)
@@ -437,11 +448,6 @@
     start = call(start_kernel, shape((ROWS, latent)), parts, vec(mesh_gain))
     state = gather_pair(start).reshape(2 * ROWS, latent)
 
-    partner_other = lax.ppermute(partner, "space", swap)
-    sent_half = lax.optimization_barrier((half, partner))[0]
-    gathered = lax.all_gather(sent_half, "section", axis=0)
-    gathered_other = lax.ppermute(gathered[2:], "space", swap)
-
     outgoing_shapes = (
         shape((chips, 2, latent)),
         shape((3 * HALO, latent)),
@@ -451,40 +457,41 @@
         pltpu.VMEM((4, latent, latent), BF),
         pltpu.VMEM((EXTRA, latent), BF),
         pltpu.VMEM((2 * ROWS + 8 * HALO + owners, latent), BF),
-        pltpu.VMEM((table_rows, latent), BF),
-        pltpu.SemaphoreType.DMA((5,)),
+        pltpu.VMEM((2, table_rows, latent), BF),
+        pltpu.VMEM((2, edges, table_rows), BF),
+        pltpu.VMEM((2, ROWS, edges), BF),
     ]
     coarse, halo, inner = call(prepare_kernel, outgoing_shapes, core, state, halo_hot, smem=1)
     for layer in range(4):
         coarse = lax.all_to_all(coarse, "space", 0, 0, tiled=True, axis_index_groups=same_core)
         coarse = coarse.reshape(owners, latent)
-        halo = gather_pair(to_next(halo))
-        inputs = (core, state, halo, inner, coarse, edges_hot, sums_hot)
-        if layer < 2:
-            state, coarse, halo, inner = call(
-                functools.partial(early_layer_kernel, layer=layer),
-                (shape(state.shape),) + outgoing_shapes,
-                *inputs, halo_hot, process_weight[0], half, partner, partner_other,
-                smem=1, hbm=4, scratch=scratch,
-            )
-        elif layer < 3:
-            state, coarse, halo, inner = call(
-                functools.partial(late_layer_kernel, layer=layer),
-                (shape(state.shape),) + outgoing_shapes,
-                *inputs, halo_hot, gathered, gathered_other,
-                smem=1, hbm=2, scratch=scratch,
-            )
+        halo = gather_pair(gather_crossing(halo))
+        if layer == 0:
+            gathered, coarse = lax.optimization_barrier((gathered, coarse))
+            gathered_other = lax.ppermute(gathered, "space", swap)
+        last = layer == 3
+        tail = decode_weight if last else halo_hot
+        weights = (gathered, gathered_other)
+        inputs = (state, halo, inner, coarse, edges_hot, sums_hot, tail) + weights
+        out = (shape((ROWS, latent)),) if last else (shape(state.shape),) + outgoing_shapes
+        out = call(
+            functools.partial(layer_kernel, layer=layer, last=last),
+            out, core, *inputs,
+            smem=1, hbm=len(inputs), hbm_out=True, limit=LAYER_LIMIT,
+            scratch=scratch
+            + [pltpu.VMEM(tail.shape[-2:], BF), pltpu.SemaphoreType.DMA((13,))]
+            + [pltpu.VMEM(o.shape, BF) for o in out]
+            + [pltpu.SemaphoreType.DMA((4,))],
+        )
+        if last:
+            keys = out[0]
         else:
-            keys = call(
-                functools.partial(last_layer_kernel, layer=layer),
-                shape((sections, ROWS, latent)),
-                *inputs, decode_weight[0], gathered, gathered_other,
-                smem=1, hbm=2, scratch=scratch,
-            )
-
-    keys = lax.all_to_all(keys, "section", 0, 0, tiled=True)
+            state, coarse, halo, inner = out
+
+    twins = [[i, i + 1] for i in range(0, sections, 2)]
+    keys = lax.all_gather(keys, "section", axis=0, axis_index_groups=twins)
     own, near, far = call(deliver_kernel, (block, block, block), core, keys, decode_senders[0], smem=1)
-    far = to_next(far)
+    far = gather_crossing(far)
     near = gather_pair(near)
     return call(
         decode_kernel,

time: 300 us -> 204 us (0.68)
  waiting for transfers between devices: 107 us -> 13.8 us
  blocking collectives: 28.4 us -> 104 us
  starting transfers between devices: 90.1 us -> 30.3 us
  local copies, waits for them, and re-layouts: 32.8 us -> 9.71 us
  Pallas kernels: 25.5 us -> 31.4 us
    all_gather x0 -> x7, blocking collectives: none -> 65.8 us  [the longest x6 59.9 us: gather_crossing(): return lax.all_gather(value, 'space', axis=0, axis_index_groups=crossings)]
    all_gather x1, waiting for transfers between devices: 60 us -> 0.55 us  [shards(): gathered = lax.all_gather(half, 'section', axis=0)]
    ppermute x9 -> x1, starting transfers between devices: 50.5 us -> 1.91 us  [shards(): gathered_other = lax.ppermute(gathered, 'space', swap)]
    ppermute x9 -> x1, waiting for transfers between devices: 34.7 us -> 0.01 us  [shards(): gathered_other = lax.ppermute(gathered, 'space', swap)]
    unnamed x115 -> x68, local copies, waits for them, and re-layouts: 25 us -> 5.63 us
    all_to_all x4 -> x3, starting transfers between devices: 34.3 us -> 23.6 us  [shards(): lax.all_to_all(coarse, 'space', 0, 0, tiled=True, axis_index_groups=same_...]
    all_to_all x1, blocking collectives: 12.2 us -> 22.4 us  [shards(): lax.all_to_all(coarse, 'space', 0, 0, tiled=True, axis_index_groups=same_...]
    pallas_call x12, Pallas kernels: 25.5 us -> 31.4 us  [call(): pl.pallas_call(kernel, out_shape=out, in_specs=specs, out_specs=jax.tree....]
  transfers between devices with their start and end apart: 15 -> 6, of which waited for: 12 -> 5; matrix products, arithmetic and copies ran while one was open for 1% -> 1% of each run, Pallas kernels for 5% -> 2%
where the time goes in v2:
time: 204 us
  blocking collectives  104 us (51%)
  Pallas kernels  31.4 us (15%)
  starting transfers between devices  30.3 us (15%)
  waiting for transfers between devices  13.8 us (7%)
  between operations  13.8 us (7%)
  local copies, waits for them, and re-layouts  9.71 us (5%)
    all_gather x6, blocking collectives, gather_crossing(): return lax.all_gather(value, 'space', axis=0, axis_index_groups=crossings)  59.9 us
    pallas_call x12, Pallas kernels, call(): pl.pallas_call(kernel, out_shape=out, in_specs=specs, out_specs=jax.tree....  31.4 us
    all_to_all x3, starting transfers between devices, shards(): lax.all_to_all(coarse, 'space', 0, 0, tiled=True, axis_index_groups=same_...  23.6 us
    all_to_all x1, blocking collectives, shards(): lax.all_to_all(coarse, 'space', 0, 0, tiled=True, axis_index_groups=same_...  22.4 us
    all_gather x8, blocking collectives, gather_pair(): return lax.all_gather(value, 'space', axis=0, axis_index_groups=pairs)  16.3 us
    all_to_all x1, waiting for transfers between devices, shards(): parts = lax.all_to_all(parts, 'section', 0, 0, tiled=True)  7.67 us
    all_gather x1, blocking collectives, shards(): keys = lax.all_gather(keys, 'section', axis=0, axis_index_groups=twins)  5.86 us
    unnamed x68, local copies, waits for them, and re-layouts  5.63 us
  transfers between devices with their start and end apart: 6, of which 5 were waited for; matrix products, arithmetic and copies ran while one was open for 1% of the time, Pallas kernels for 2%

profile of v2, /device:TPU:2, one launch (start us, length us, event | category | flops | bytes accessed | tf_op | source)
XLA Modules:
  0.0 203.6 jit_solution(16399221297520693892)
XLA Ops:
  14.0 2.0 all-gather
  16.0 15.0 %all-gather.1 = bf16[256,512]{1,0:T(8,128)(2,1)S(1)} all-gather(bf16[128,512]{1,0:T(8,128)(2,1)S(1)} %get-tuple-element.36), channel_id=3, replica_groups={{1,2},{3,4},{5,6},{7,8},{9,10},{11,12},{13,14},{15,16},{17,18},{19,20},..., dimensions={0}, use_global_device_ids=true | all-gather | bytes 393216 | tf_op jit(solution)/shard_map/all_gather | solution.py:388
  32.9 4.8 %all-to-all-start = ((bf16[4,128,512]{2,1,0:T(8,128)(2,1)}), bf16[4,128,512]{2,1,0:T(8,128)(2,1)S(1)}, u32[]{:S(2)}, u32[]{:S(2)}) async-start(bf16[4,128,512]{2,1,0:T(8,128)(2,1)} %shard_map.237), calls=%async_computation | async-start | bytes 1048576 | tf_op jit(solution)/shard_map/all_to_all | solution.py:447
  42.3 7.7 %all-to-all-done.parts = bf16[4,128,512]{2,1,0:T(8,128)(2,1)S(1)} async-done(((bf16[4,128,512]{2,1,0:T(8,128)(2,1)}), bf16[4,128,512]{2,1,0:T(8,128)(2,1)S(1)}, u32[]{:S(2)}, u32[]{:S(2)}) %all-to-all-start) | async-done | bytes 524320 | tf_op jit(solution)/shard_map/all_to_all | solution.py:447
  50.2 2.0 all-gather.2.state.refs_0_
  53.0 22.4 %all_to_all.25 = bf16[64,2,512]{2,1,0:T(2,128)(2,1)S(1)} all-to-all(bf16[64,2,512]{2,1,0:T(2,128)(2,1)S(1)} %get-tuple-element.40), channel_id=1, replica_groups={{0,2,4,6,8,10,12,14,16,18,20,22,24,26,28,30,32,34,36,38,40,42,44,46,48,..., dimensions={0} | all-to-all | bytes 262144 | tf_op jit(solution)/shard_map/all_to_all | solution.py:466
  78.5 10.1 %all-gather.4 = bf16[96,512]{1,0:T(8,128)(2,1)S(1)} all-gather(bf16[48,512]{1,0:T(8,128)(2,1)S(1)} %get-tuple-element.38), channel_id=6, replica_groups={{1,2},{3,4},{5,6},{7,8},{9,10},{11,12},{13,14},{15,16},{17,18},{19,20},..., dimensions={0}, use_global_device_ids=true | all-gather | bytes 147456 | tf_op jit(solution)/shard_map/all_gather | solution.py:388
  88.5 2.1 %all-gather.5 = bf16[4,48,512]{2,1,0:T(8,128)(2,1)} all-gather(bf16[2,48,512]{2,1,0:T(8,128)(2,1)S(1)} %bitcast.86), channel_id=7, replica_groups={{0,1},{2,3},{4,5},{6,7},{8,9},{10,11},{12,13},{14,15},{16,17},{18,19},{..., dimensions={0}, use_global_device_ids=true | all-gather | bytes 294912 | tf_op jit(solution)/shard_map/all_gather | solution.py:385
  90.6 5.6 %shard_map.241 = (bf16[256,512]{1,0:T(8,128)(2,1)}, bf16[64,2,512]{2,1,0:T(2,128)(2,1)}, bf16[48,512]{1,0:T(8,128)(2,1)}, bf16[32,512]{1,0:T(8,128)(2,1)}) custom-call(s32[2]{0:T(128)} %copy-done.8, bf16[256,512]{1,0:T(8,128)(2,1)} %copy-done.3, bf16[2,2,48,512]{3,2,1,0:T(8,128)(2,1)} %bitcast.85, bf16[32,512]{1,0:T(8,128)(2,1)} %copy-done.10, ...), custom_call_target="tpu_custom_call" | custom-call | flops 1000000 | bytes 1000000 | tf_op jit(solution)/shard_map/pallas_call | solution.py:76
  96.2 8.3 %all-to-all-start.2 = ((bf16[64,2,512]{2,1,0:T(2,128)(2,1)}), bf16[64,2,512]{2,1,0:T(2,128)(2,1)S(1)}, u32[]{:S(2)}, u32[]{:S(2)}) async-start(bf16[64,2,512]{2,1,0:T(2,128)(2,1)} %get-tuple-element.48), calls=%async_computation.2 | async-start | bytes 262144 | tf_op jit(solution)/shard_map/all_to_all | solution.py:466
  104.5 8.8 %all-gather.7 = bf16[96,512]{1,0:T(8,128)(2,1)S(1)} all-gather(bf16[48,512]{1,0:T(8,128)(2,1)} %get-tuple-element.46), channel_id=9, replica_groups={{1,2},{3,4},{5,6},{7,8},{9,10},{11,12},{13,14},{15,16},{17,18},{19,20},..., dimensions={0}, use_global_device_ids=true | all-gather | bytes 147456 | tf_op jit(solution)/shard_map/all_gather | solution.py:388
  113.4 2.1 %all-gather.8 = bf16[4,48,512]{2,1,0:T(8,128)(2,1)} all-gather(bf16[2,48,512]{2,1,0:T(8,128)(2,1)S(1)} %bitcast.87), channel_id=10, replica_groups={{0,1},{2,3},{4,5},{6,7},{8,9},{10,11},{12,13},{14,15},{16,17},{18,19},{..., dimensions={0}, use_global_device_ids=true | all-gather | bytes 294912 | tf_op jit(solution)/shard_map/all_gather | solution.py:385
  118.1 5.6 %shard_map.242 = (bf16[256,512]{1,0:T(8,128)(2,1)}, bf16[64,2,512]{2,1,0:T(2,128)(2,1)}, bf16[48,512]{1,0:T(8,128)(2,1)}, bf16[32,512]{1,0:T(8,128)(2,1)}) custom-call(s32[2]{0:T(128)} %copy-done.8, bf16[256,512]{1,0:T(8,128)(2,1)} %get-tuple-element.45.refs_0_, bf16[2,2,48,512]{3,2,1,0:T(8,128)(2,1)} %bitcast.83, ...), custom_call_target="tpu_custom_call" | custom-call | flops 1000000 | bytes 1000000 | tf_op jit(solution)/shard_map/pallas_call | solution.py:76
  123.6 7.6 %all-to-all-start.3 = ((bf16[64,2,512]{2,1,0:T(2,128)(2,1)}), bf16[64,2,512]{2,1,0:T(2,128)(2,1)S(1)}, u32[]{:S(2)}, u32[]{:S(2)}) async-start(bf16[64,2,512]{2,1,0:T(2,128)(2,1)} %get-tuple-element.52), calls=%async_computation.3 | async-start | bytes 262144 | tf_op jit(solution)/shard_map/all_to_all | solution.py:466
  131.2 8.9 %all-gather.9 = bf16[96,512]{1,0:T(8,128)(2,1)S(1)} all-gather(bf16[48,512]{1,0:T(8,128)(2,1)} %get-tuple-element.50), channel_id=11, replica_groups={{1,2},{3,4},{5,6},{7,8},{9,10},{11,12},{13,14},{15,16},{17,18},{19,20},..., dimensions={0}, use_global_device_ids=true | all-gather | bytes 147456 | tf_op jit(solution)/shard_map/all_gather | solution.py:388
  140.1 2.2 %all-gather.10 = bf16[4,48,512]{2,1,0:T(8,128)(2,1)} all-gather(bf16[2,48,512]{2,1,0:T(8,128)(2,1)S(1)} %bitcast.88), channel_id=12, replica_groups={{0,1},{2,3},{4,5},{6,7},{8,9},{10,11},{12,13},{14,15},{16,17},{18,19},{..., dimensions={0}, use_global_device_ids=true | all-gather | bytes 294912 | tf_op jit(solution)/shard_map/all_gather | solution.py:385
  144.8 5.7 %shard_map.243 = (bf16[256,512]{1,0:T(8,128)(2,1)}, bf16[64,2,512]{2,1,0:T(2,128)(2,1)}, bf16[48,512]{1,0:T(8,128)(2,1)}, bf16[32,512]{1,0:T(8,128)(2,1)}) custom-call(s32[2]{0:T(128)} %copy-done.8, bf16[256,512]{1,0:T(8,128)(2,1)} %get-tuple-element.49.refs_0_, bf16[2,2,48,512]{3,2,1,0:T(8,128)(2,1)} %bitcast.82, ...), custom_call_target="tpu_custom_call" | custom-call | flops 1000000 | bytes 1000000 | tf_op jit(solution)/shard_map/pallas_call | solution.py:76
  150.5 7.7 %all-to-all-start.4 = ((bf16[64,2,512]{2,1,0:T(2,128)(2,1)}), bf16[64,2,512]{2,1,0:T(2,128)(2,1)S(1)}, u32[]{:S(2)}, u32[]{:S(2)}) async-start(bf16[64,2,512]{2,1,0:T(2,128)(2,1)} %get-tuple-element.56), calls=%async_computation.4 | async-start | bytes 262144 | tf_op jit(solution)/shard_map/all_to_all | solution.py:466
  158.4 8.8 %all-gather.11 = bf16[96,512]{1,0:T(8,128)(2,1)S(1)} all-gather(bf16[48,512]{1,0:T(8,128)(2,1)} %get-tuple-element.54), channel_id=13, replica_groups={{1,2},{3,4},{5,6},{7,8},{9,10},{11,12},{13,14},{15,16},{17,18},{19,20},..., dimensions={0}, use_global_device_ids=true | all-gather | bytes 147456 | tf_op jit(solution)/shard_map/all_gather | solution.py:388
  167.1 2.1 %all-gather.12 = bf16[4,48,512]{2,1,0:T(8,128)(2,1)} all-gather(bf16[2,48,512]{2,1,0:T(8,128)(2,1)S(1)} %bitcast.89), channel_id=14, replica_groups={{0,1},{2,3},{4,5},{6,7},{8,9},{10,11},{12,13},{14,15},{16,17},{18,19},{..., dimensions={0}, use_global_device_ids=true | all-gather | bytes 294912 | tf_op jit(solution)/shard_map/all_gather | solution.py:385
  171.8 5.7 %shard_map.244 = bf16[128,512]{1,0:T(8,128)(2,1)} custom-call(s32[2]{0:T(128)} %copy-done.8, bf16[256,512]{1,0:T(8,128)(2,1)} %get-tuple-element.53.refs_0_, bf16[2,2,48,512]{3,2,1,0:T(8,128)(2,1)} %bitcast.84, bf16[32,512]{1,0:T(8,128)(2,1)} %get-tuple-element.55.refs_2_, bf16[128,512]{1,0:T(8,128)(2,1)} %reshape.47.refs_3_, bf16[2,448,512]{2,1,0:T(8,128)(2,1)} %copy-done, ...), custom_call_target="tpu_custom_call" | custom-call | flops 1000000 | bytes 1000000 | tf_op jit(solution)/shard_map/pallas_call | solution.py:76
  177.5 5.9 %all-gather.13 = bf16[256,512]{1,0:T(8,128)(2,1)S(1)} all-gather(bf16[128,512]{1,0:T(8,128)(2,1)} %shard_map.244), channel_id=15, replica_groups={{0,128},{256,384},{1,129},{257,385},{2,130},{258,386},{3,131},{259,387}..., dimensions={0}, use_global_device_ids=true | all-gather | bytes 393216 | tf_op jit(solution)/shard_map/all_gather | solution.py:492
  184.2 2.0 all-gather.14
  186.2 8.4 %all-gather.15 = bf16[256,512]{1,0:T(8,128)(2,1)S(1)} all-gather(bf16[128,512]{1,0:T(8,128)(2,1)S(1)} %get-tuple-element.59), channel_id=17, replica_groups={{1,2},{3,4},{5,6},{7,8},{9,10},{11,12},{13,14},{15,16},{17,18},{19,20},..., dimensions={0}, use_global_device_ids=true | all-gather | bytes 393216 | tf_op jit(solution)/shard_map/all_gather | solution.py:388
  (103 shorter events, 28.8 us)
Async XLA Ops:
  6.5 70.0 %all-gather.18.cloned.1.call-start = ((), (), s32[]{:S(2)}) async-start(), calls=%async_computation.5 | async-start | bytes 5570560 | tf_op jit(solution)/shard_map/all_gather | solution.py:407
  6.6 45.6 %copy-start.8 = (s32[2]{0:T(128)}, s32[2]{0:T(128)S(1)}, u32[]{:S(2)}) copy-start(s32[2]{0:T(128)S(1)} %pad_add_fusion.core) | copy-start | bytes 28
  10.4 20.6 %copy-start.12 = (f32[4,512]{1,0:T(4,128)S(1)}, f32[4,512]{1,0:T(4,128)}, u32[]{:S(2)}) copy-start(f32[4,512]{1,0:T(4,128)} %weight.2) | copy-start | bytes 24580
  10.4 20.6 %copy-start.16 = (f32[512]{0:T(512)S(1)}, f32[512]{0:T(512)}, u32[]{:S(2)}) copy-start(f32[512]{0:T(512)} %param.30) | copy-start | bytes 6148
  10.4 20.6 %copy-start.21 = (s32[1,1,192]{2,1,0:T(1,128)S(1)}, s32[1,1,192]{2,1,0:T(1,128)}, u32[]{:S(2)}) copy-start(s32[1,1,192]{2,1,0:T(1,128)} %param.41) | copy-start | bytes 2308
  10.4 27.3 %copy-start.26 = (s32[1,64]{1,0:T(1,128)S(1)}, s32[1,64]{1,0:T(1,128)}, u32[]{:S(2)}) copy-start(s32[1,64]{1,0:T(1,128)} %param.43) | copy-start | bytes 772
  10.4 27.7 %copy-start.27 = (f32[4,1,448]{2,1,0:T(1,128)S(1)}, f32[4,1,448]{2,1,0:T(1,128)}, u32[]{:S(2)}) copy-start(f32[4,1,448]{2,1,0:T(1,128)} %param.46) | copy-start | bytes 21508
  10.4 27.7 %copy-start.30 = (s32[1,448]{1,0:T(1,128)S(1)}, s32[1,448]{1,0:T(1,128)}, u32[]{:S(2)}) copy-start(s32[1,448]{1,0:T(1,128)} %param.45) | copy-start | bytes 5380
  10.5 27.7 %copy-start.31 = (s32[1,448]{1,0:T(1,128)S(1)}, s32[1,448]{1,0:T(1,128)}, u32[]{:S(2)}) copy-start(s32[1,448]{1,0:T(1,128)} %param.44) | copy-start | bytes 5380
  10.5 39.5 %copy-start.17 = (f32[512]{0:T(512)S(1)}, f32[512]{0:T(512)}, u32[]{:S(2)}) copy-start(f32[512]{0:T(512)} %param.31) | copy-start | bytes 6148
  32.9 17.0 %all-to-all-start = ((bf16[4,128,512]{2,1,0:T(8,128)(2,1)}), bf16[4,128,512]{2,1,0:T(8,128)(2,1)S(1)}, u32[]{:S(2)}, u32[]{:S(2)}) async-start(bf16[4,128,512]{2,1,0:T(8,128)(2,1)} %shard_map.237), calls=%async_computation | async-start | bytes 1048576 | tf_op jit(solution)/shard_map/all_to_all | solution.py:447
  42.3 48.3 %copy-start.5 = (bf16[128,256]{1,0:T(8,128)(2,1)}, bf16[128,256]{1,0:T(8,128)(2,1)S(1)}, u32[]{:S(2)}) copy-start(bf16[128,256]{1,0:T(8,128)(2,1)S(1)} %get-tuple-element.37.halo_hot.refs_6_) | copy-start | bytes 196612
  52.2 38.4 %copy-start.3 = (bf16[256,512]{1,0:T(8,128)(2,1)}, bf16[256,512]{1,0:T(8,128)(2,1)S(1)}, u32[]{:S(2)}) copy-start(bf16[256,512]{1,0:T(8,128)(2,1)S(1)} %all-gather.2.state.refs_0_) | copy-start | bytes 786436
  52.9 37.7 %copy-start.10 = (bf16[32,512]{1,0:T(8,128)(2,1)}, bf16[32,512]{1,0:T(8,128)(2,1)S(1)}, u32[]{:S(2)}) copy-start(bf16[32,512]{1,0:T(8,128)(2,1)S(1)} %get-tuple-element.39.refs_2_) | copy-start | bytes 98308
  76.6 14.0 %collective-permute-start = (bf16[4,1088,512]{2,1,0:T(8,128)(2,1)}, bf16[4,1088,512]{2,1,0:T(8,128)(2,1)}, u32[]{:S(2)}, u32[]{:S(2)}) collective-permute-start(bf16[4,1088,512]{2,1,0:T(8,128)(2,1)} %bitcast.77), channel_id=1, source_target_pairs={{0,1},{1,0},{2,3},{3,2},{4,5},{5,4},{6,7},{7,6},{8,9},{9,8},{10,11... | collective-permute-start | bytes 13369352 | tf_op jit(solution)/shard_map/ppermute | solution.py:471
  96.2 21.2 %all-to-all-start.2 = ((bf16[64,2,512]{2,1,0:T(2,128)(2,1)}), bf16[64,2,512]{2,1,0:T(2,128)(2,1)S(1)}, u32[]{:S(2)}, u32[]{:S(2)}) async-start(bf16[64,2,512]{2,1,0:T(2,128)(2,1)} %get-tuple-element.48), calls=%async_computation.2 | async-start | bytes 262144 | tf_op jit(solution)/shard_map/all_to_all | solution.py:466
  123.6 20.5 %all-to-all-start.3 = ((bf16[64,2,512]{2,1,0:T(2,128)(2,1)}), bf16[64,2,512]{2,1,0:T(2,128)(2,1)S(1)}, u32[]{:S(2)}, u32[]{:S(2)}) async-start(bf16[64,2,512]{2,1,0:T(2,128)(2,1)} %get-tuple-element.52), calls=%async_computation.3 | async-start | bytes 262144 | tf_op jit(solution)/shard_map/all_to_all | solution.py:466
  144.8 13.4 %copy-start.25 = (bf16[512,227]{0,1:T(8,128)(2,1)S(1)}, bf16[512,227]{0,1:T(8,128)(2,1)}, u32[]{:S(2)}) copy-start(bf16[512,227]{0,1:T(8,128)(2,1)} %param.39) | copy-start | bytes 697348
  144.8 13.5 %copy-start.29 = (f32[4,1,1,192]{3,2,1,0:T(1,128)S(1)}, f32[4,1,1,192]{3,2,1,0:T(1,128)}, u32[]{:S(2)}) copy-start(f32[4,1,1,192]{3,2,1,0:T(1,128)} %param.49) | copy-start | bytes 9220
  150.5 20.5 %all-to-all-start.4 = ((bf16[64,2,512]{2,1,0:T(2,128)(2,1)}), bf16[64,2,512]{2,1,0:T(2,128)(2,1)S(1)}, u32[]{:S(2)}, u32[]{:S(2)}) async-start(bf16[64,2,512]{2,1,0:T(2,128)(2,1)} %get-tuple-element.56), calls=%async_computation.4 | async-start | bytes 262144 | tf_op jit(solution)/shard_map/all_to_all | solution.py:466
  171.8 11.6 %copy-start.22 = (s32[1,1,192]{2,1,0:T(1,128)S(1)}, s32[1,1,192]{2,1,0:T(1,128)}, u32[]{:S(2)}) copy-start(s32[1,1,192]{2,1,0:T(1,128)} %param.47) | copy-start | bytes 2308
  171.8 22.8 %copy-start.13 = (f32[4,512]{1,0:T(4,128)S(1)}, f32[4,512]{1,0:T(4,128)}, u32[]{:S(2)}) copy-start(f32[4,512]{1,0:T(4,128)} %weight.3) | copy-start | bytes 24580
  171.8 22.8 %copy-start.18 = (f32[512]{0:T(512)S(1)}, f32[512]{0:T(512)}, u32[]{:S(2)}) copy-start(f32[512]{0:T(512)} %param.38) | copy-start | bytes 6148
  171.8 22.8 %copy-start.23 = (s32[1,1,192]{2,1,0:T(1,128)S(1)}, s32[1,1,192]{2,1,0:T(1,128)}, u32[]{:S(2)}) copy-start(s32[1,1,192]{2,1,0:T(1,128)} %param.48) | copy-start | bytes 2308
  (14 other events, 35.4 us)
Sparse Core Ops, SparseCore 0:
  12.4 64.1 all-gather.17

commit v3 on v2

--- a/solution.py
+++ b/solution.py
@@ -14,7 +14,8 @@
 EXTRA = 64
 NODE_BIAS, GAIN = 32, 35
 SMALL_LIMIT = 16 * 1024 * 1024
-LAYER_LIMIT = 63_000_000
+LAYER_LIMIT = 54000000
+PACK_LIMIT = 64_900_000
 
 
 def silu(v):
@@ -62,13 +63,15 @@
     return dot_t(feature_parts(features).astype(BF), weight_parts(weight).astype(BF))
 
 
-def call(kernel, out, *args, smem=0, hbm=0, scratch=(), hbm_out=False, limit=SMALL_LIMIT):
+def core_index():
+    return lax.axis_index("space") % 2
+
+
+def call(kernel, out, *args, hbm=0, scratch=(), hbm_out=False, limit=SMALL_LIMIT):
     count = len(args)
     specs = []
     for position in range(count):
-        if position < smem:
-            specs.append(pl.BlockSpec(memory_space=pltpu.SMEM))
-        elif position >= count - hbm:
+        if position >= count - hbm:
             specs.append(pl.BlockSpec(memory_space=pltpu.HBM))
         else:
             specs.append(pl.BlockSpec(memory_space=pltpu.VMEM))
@@ -88,22 +91,35 @@
     return jax.ShapeDtypeStruct(dims, dtype)
 
 
-def pack_weights_kernel(core, edge_from, bias_from, gain_from, weight, out, edge_weight, bias, gain, packed, sems):
+def pack_weights_kernel(edge_from, bias_from, gain_from, weight, out, edge_weight, bias, gain, packed, sems):
     size = weight.shape[1]
     half = 2 * size
     vectors = [
-        pltpu.make_async_copy(source, target, sems.at[2 + i])
+        pltpu.make_async_copy(source, target, sems.at[i])
         for i, (source, target) in enumerate(
             ((edge_from, edge_weight), (bias_from, bias), (gain_from, gain))
         )
     ]
+    pieces = 4
+    piece = half // pieces
+    first = 2 * core_index()
+    places = [pl.ds(i * piece, piece) for i in range(pieces)]
     matrices = [
         pltpu.make_async_copy(
-            weight.at[2 * core[0] + m], packed.at[pl.ds(m * size, size)], sems.at[m]
+            weight.at[first + i * piece // size, pl.ds(i * piece % size, piece)],
+            packed.at[places[i]],
+            sems.at[3 + i],
         )
-        for m in range(2)
+        for i in range(pieces)
+    ]
+    packs = [
+        pltpu.make_async_copy(packed.at[place], out.at[place], sems.at[3 + pieces + i])
+        for i, place in enumerate(places + [pl.ds(half, EXTRA)])
     ]
     for copy in vectors + matrices:
+        copy.start()
+    for arrival, copy in zip(matrices, packs):
+        arrival.wait()
         copy.start()
     for copy in vectors:
         copy.wait()
@@ -121,11 +137,9 @@
         axis=0,
     )
     packed[half:] = rows.astype(BF)
-    for copy in matrices:
+    packs[pieces].start()
+    for copy in packs:
         copy.wait()
-    whole = pltpu.make_async_copy(packed, out, sems.at[0])
-    whole.start()
-    whole.wait()
 
 
 def setup_kernel(meta, edges_out, sums_out, halo_out, *, coarse):
@@ -163,15 +177,15 @@
     halo_out[...] = jnp.transpose(hot).astype(BF)
 
 
-def embed_kernel(core, x, embed_weight, embed_bias, encode_weight, query_weight, senders, own, near, far, queries):
+def embed_kernel(x, embed_weight, embed_bias, encode_weight, query_weight, senders, own, near, far, queries):
     latent = silu(dot(x[...], embed_weight[...]) + embed_bias[...]).astype(BF)
     keys = dot(latent, encode_weight[...]).astype(BF)
-    send_blocks(core, keys, senders, own, near, far)
+    send_blocks(keys, senders, own, near, far)
     queries[...] = dot(latent, query_weight[1]).astype(BF)
 
 
-def send_blocks(core, keys, senders, own, near, far):
-    first = core[0] == 0
+def send_blocks(keys, senders, own, near, far):
+    first = core_index() == 0
     cap = senders.shape[1] // 3
     hot = hot_rows(senders[...], ROWS)
     for sample in range(2):
@@ -182,8 +196,8 @@
         far[out] = jnp.where(first, rows[2 * cap :], rows[cap : 2 * cap])
 
 
-def arrived_rows(core, own, near, far, sample):
-    first = core[0] == 0
+def arrived_rows(own, near, far, sample):
+    first = core_index() == 0
     cap = own.shape[0] // 2
     at = pl.ds(sample * cap, cap)
     from_near = jnp.where(first, near[1, at], near[0, at])
@@ -194,11 +208,11 @@
     ).astype(F32)
 
 
-def message_kernel(core, own, near, far, features, weight, bias, receivers, out):
+def message_kernel(own, near, far, features, weight, bias, receivers, out):
     edge = edge_term(features[...], weight[...]) + bias[...]
     hot = hot_rows(receivers[...], ROWS)
     for sample in range(2):
-        rows = arrived_rows(core, own, near, far, sample)
+        rows = arrived_rows(own, near, far, sample)
         message = silu(rows + edge).astype(BF)
         sums = dot(hot, message).astype(BF)
         out[sample] = sums
@@ -212,39 +226,34 @@
     out[...] = layer_norm(total, gain[...]).astype(BF)
 
 
-def outgoing(core, state, halo_hot, coarse_out, halo_out, inner_out):
+def outgoing(state, halo_hot, coarse_out, halo_out, inner_out):
     rows = dot(halo_hot[...], state).astype(BF)
-    halo_out[...] = jnp.where(core[0] == 0, rows[3 * HALO : 6 * HALO], rows[: 3 * HALO])
+    halo_out[...] = jnp.where(core_index() == 0, rows[3 * HALO : 6 * HALO], rows[: 3 * HALO])
     inner_out[...] = rows[6 * HALO :]
     pair = jnp.concatenate([state[0:1].astype(F32), state[ROWS : ROWS + 1].astype(F32)], axis=0)
     coarse_out[...] = jnp.broadcast_to(pair.astype(BF)[None], coarse_out.shape)
 
 
-def prepare_kernel(core, state, halo_hot, coarse_out, halo_out, inner_out):
-    outgoing(core, state[...], halo_hot, coarse_out, halo_out, inner_out)
-
-
-def fetch_weights(core, wbuf, ebuf, sems, mine, other):
-    size = wbuf.shape[1]
-
-    def start(m):
-        at = pl.ds((m % 2) * size, size)
-
-        @pl.when(core[0] == m // 2)
-        def _():
-            pltpu.make_async_copy(mine.at[at], wbuf.at[m], sems.at[m]).start()
-
-        @pl.when(core[0] != m // 2)
-        def _():
-            pltpu.make_async_copy(other.at[at], wbuf.at[m], sems.at[m]).start()
-
-        return pltpu.make_async_copy(mine.at[at], wbuf.at[m], sems.at[m])
-
-    tail = pltpu.make_async_copy(mine.at[pl.ds(2 * size, EXTRA)], ebuf, sems.at[4])
-    return start, tail
-
-
-def layer_kernel(core, *refs, layer, last):
+def prepare_kernel(state, halo_hot, coarse_out, halo_out, inner_out):
+    outgoing(state[...], halo_hot, coarse_out, halo_out, inner_out)
+
+
+def fetch(m, target, sem, mine, other):
+    size = target.shape[0]
+    at = pl.ds((m % 2) * size, size)
+
+    @pl.when(core_index() == m // 2)
+    def _():
+        pltpu.make_async_copy(mine.at[at], target, sem).start()
+
+    @pl.when(core_index() != m // 2)
+    def _():
+        pltpu.make_async_copy(other.at[at], target, sem).start()
+
+    return pltpu.make_async_copy(mine.at[at], target, sem)
+
+
+def layer_kernel(*refs, layer, last):
     refs = list(refs)
 
     def take(count):
@@ -252,50 +261,30 @@
         del refs[:count]
         return taken
 
-    state, halo, inner, coarse, edges_hot, sums_hot, tail_from = take(7)
+    state, halo, inner, coarse, hot, sums, tail_weight = take(7)
     mine, other = take(2)
     outs = take(1 if last else 4)
-    wbuf, ebuf, sources, table, hot, sums, tail_weight, sems = take(8)
-    staged = take(len(outs))
-    (out_sems,) = refs
-
+    wbuf, ebuf, sources, table, sems = refs
+    size = wbuf.shape[1]
+    here = mine.at[layer]
+    there = other if layer == 0 else other.at[layer]
+    first = [fetch(m, wbuf.at[m], sems.at[m], here, there) for m in range(2)]
+    vectors = pltpu.make_async_copy(here.at[pl.ds(2 * size, EXTRA)], ebuf, sems.at[4])
+    vectors.start()
+    second = [fetch(m, wbuf.at[m], sems.at[m], here, there) for m in (3, 2)]
     at_halo = 2 * ROWS
     at_inner = at_halo + 6 * HALO
     at_coarse = at_inner + 2 * HALO
     coarse_rows = coarse.shape[0]
-    in_place = [
-        pltpu.make_async_copy(source, sources.at[pl.ds(at, count)], sems.at[5 + i])
-        for i, (source, at, count) in enumerate(
-            (
-                (state, 0, 2 * ROWS),
-                (halo.at[0, 0], at_halo, 3 * HALO),
-                (halo.at[1, 1], at_halo + 3 * HALO, 3 * HALO),
-                (inner, at_inner, 2 * HALO),
-                (coarse, at_coarse, coarse_rows),
-            )
-        )
-    ]
-    for copy in in_place:
-        copy.start()
-    later = [
-        pltpu.make_async_copy(edges_hot, hot, sems.at[10]),
-        pltpu.make_async_copy(sums_hot, sums, sems.at[11]),
-        pltpu.make_async_copy(tail_from.at[0] if last else tail_from, tail_weight, sems.at[12]),
-    ]
-    start, vectors = fetch_weights(core, wbuf, ebuf, sems, mine.at[layer], other.at[layer])
-    waits = [start(0), start(1)]
-    vectors.start()
-    later[0].start()
-    later[1].start()
-    waits += [start(2), start(3), vectors]
-    later[2].start()
-
-    for copy in in_place:
-        copy.wait()
-    waits[0].wait()
+    sources[0:at_halo] = state[...]
+    sources[at_halo : at_halo + 3 * HALO] = halo[0, 0]
+    sources[at_halo + 3 * HALO : at_inner] = halo[1, 1]
+    sources[at_inner:at_coarse] = inner[...]
+    sources[at_coarse:] = coarse[...]
+    first[0].wait()
     keys = dot(sources[...], wbuf[0]).astype(BF)
-    waits[1].wait()
-    old = sources[0:at_halo]
+    first[1].wait()
+    old = state[...]
     target = dot(old, wbuf[1]).astype(BF)
     up, down = at_halo, at_halo + 3 * HALO
     halo_from = (
@@ -303,9 +292,7 @@
         (at_inner + HALO, down, up + 2 * HALO, down + 2 * HALO),
     )
     at_target = ROWS + 4 * HALO + coarse_rows
-    waits[4].wait()
-    later[0].wait()
-    later[1].wait()
+    vectors.wait()
     nodes = []
     for owner in range(2):
         table[owner, 0:ROWS] = keys[owner * ROWS : (owner + 1) * ROWS]
@@ -318,9 +305,9 @@
         hidden = silu(dot(hot[owner], table[owner])).astype(BF)
         nodes.append(dot(sums[owner], hidden).astype(BF))
     node_in = jnp.concatenate(nodes, axis=0)
-    waits[3].wait()
+    second[0].wait()
     kept = dot(old, wbuf[3])
-    waits[2].wait()
+    second[1].wait()
 
     def vector(at):
         return (ebuf[at : at + 1].astype(F32) + ebuf[at + 1 : at + 2].astype(F32)) + ebuf[
@@ -329,33 +316,26 @@
 
     update = silu(dot(node_in, wbuf[2]) + kept + vector(NODE_BIAS))
     new = (old.astype(F32) + layer_norm(update, vector(GAIN))).astype(BF)
-    later[2].wait()
     if last:
-        rows = jnp.where(core[0] == 0, new[:ROWS], new[ROWS:])
-        projected = dot(rows, tail_weight[...]).astype(BF)
-        staged[0][...] = projected
+        rows = jnp.where(core_index() == 0, new[:ROWS], new[ROWS:])
+        outs[0][...] = dot(rows, tail_weight[0]).astype(BF)
     else:
-        staged[0][...] = new
-        outgoing(core, new, tail_weight, *staged[1:])
-    sent = [pltpu.make_async_copy(a, b, out_sems.at[i]) for i, (a, b) in enumerate(zip(staged, outs))]
-    for copy in sent:
-        copy.start()
-    for copy in sent:
-        copy.wait()
-
-
-def deliver_kernel(core, keys, senders, own, near, far):
+        outs[0][...] = new
+        outgoing(new, tail_weight, *outs[1:])
+
+
+def deliver_kernel(keys, senders, own, near, far):
     both = jnp.concatenate([keys[0], keys[1]], axis=0)
-    send_blocks(core, both, senders, own, near, far)
-
-
-def decode_kernel(core, own, near, far, queries, features, weight, bias, receivers, x, out_weight, out):
+    send_blocks(both, senders, own, near, far)
+
+
+def decode_kernel(own, near, far, queries, features, weight, bias, receivers, x, out_weight, out):
     edge = edge_term(features[...], weight[...]) + bias[...]
     hot = hot_rows(receivers[...], ROWS)
     width = out_weight.shape[1]
     for sample in range(2):
         at = pl.ds(sample * ROWS, ROWS)
-        rows = arrived_rows(core, own, near, far, sample)
+        rows = arrived_rows(own, near, far, sample)
         hidden = silu(rows + dot_t(hot, queries[at]) + edge).astype(BF)
         total = dot(hot, hidden).astype(BF)
         change = dot(total, out_weight[...])
@@ -373,9 +353,7 @@
     owners = lax.axis_size("space")
     chips = owners // 2
     sections = lax.axis_size("section")
-    section = lax.axis_index("section")
     core_id = lax.axis_index("space") % 2
-    core = jnp.stack([core_id, section % 2]).astype(jnp.int32)
     pairs = [[2 * k, 2 * k + 1] for k in range(chips)]
     same_core = [[2 * k + c for k in range(chips)] for c in range(2)]
     crossings = [[2 * k + 1, (2 * k + 2) % owners] for k in range(chips)]
@@ -394,14 +372,14 @@
     half = call(
         pack_weights_kernel,
         shape((half_rows, latent)),
-        core, process_edge_weight[0], process_bias[0], process_gain, process_weight[0],
-        smem=1, hbm=4, hbm_out=True,
+        process_edge_weight[0], process_bias[0], process_gain, process_weight[0],
+        hbm=4, hbm_out=True, limit=PACK_LIMIT,
         scratch=[
             pltpu.VMEM(process_edge_weight.shape[1:], F32),
             pltpu.VMEM(process_bias.shape[1:], F32),
             pltpu.VMEM(process_gain.shape, F32),
             pltpu.VMEM((half_rows, latent), BF),
-            pltpu.SemaphoreType.DMA((5,)),
+            pltpu.SemaphoreType.DMA((12,)),
         ],
     )
     gathered = lax.all_gather(half, "section", axis=0)
@@ -413,8 +391,7 @@
     own, near, far, queries = call(
         embed_kernel,
         (block, block, block, shape((samples * grid_rows, latent))),
-        core, x, embed_weight, vec(embed_bias), encode_weight, decode_weight, encode_senders[0],
-        smem=1,
+        x, embed_weight, vec(embed_bias), encode_weight, decode_weight, encode_senders[0],
     )
     far = gather_crossing(far)
     near = gather_pair(near)
@@ -441,8 +418,7 @@
     parts = call(
         message_kernel,
         shape((sections, ROWS, latent)),
-        core, own, near, far, encode_features[:, 0, 0, :], encode_edge_weight, vec(encode_bias), encode_receivers[0],
-        smem=1,
+        own, near, far, encode_features[:, 0, 0, :], encode_edge_weight, vec(encode_bias), encode_receivers[0],
     )
     parts = lax.all_to_all(parts, "section", 0, 0, tiled=True)
     start = call(start_kernel, shape((ROWS, latent)), parts, vec(mesh_gain))
@@ -458,47 +434,47 @@
         pltpu.VMEM((EXTRA, latent), BF),
         pltpu.VMEM((2 * ROWS + 8 * HALO + owners, latent), BF),
         pltpu.VMEM((2, table_rows, latent), BF),
-        pltpu.VMEM((2, edges, table_rows), BF),
-        pltpu.VMEM((2, ROWS, edges), BF),
+        pltpu.SemaphoreType.DMA((5,)),
     ]
-    coarse, halo, inner = call(prepare_kernel, outgoing_shapes, core, state, halo_hot, smem=1)
+    coarse, halo, inner = call(prepare_kernel, outgoing_shapes, state, halo_hot)
     for layer in range(4):
         coarse = lax.all_to_all(coarse, "space", 0, 0, tiled=True, axis_index_groups=same_core)
         coarse = coarse.reshape(owners, latent)
         halo = gather_pair(gather_crossing(halo))
         if layer == 0:
-            gathered, coarse = lax.optimization_barrier((gathered, coarse))
-            gathered_other = lax.ppermute(gathered, "space", swap)
+            gathered, halo, coarse = lax.optimization_barrier((gathered, halo, coarse))
+            gathered_other = lax.ppermute(gathered[0], "space", swap)
         last = layer == 3
         tail = decode_weight if last else halo_hot
         weights = (gathered, gathered_other)
         inputs = (state, halo, inner, coarse, edges_hot, sums_hot, tail) + weights
-        out = (shape((ROWS, latent)),) if last else (shape(state.shape),) + outgoing_shapes
+        if last:
+            out = (shape((ROWS, latent)),)
+        else:
+            out = (shape(state.shape),) + outgoing_shapes
         out = call(
             functools.partial(layer_kernel, layer=layer, last=last),
-            out, core, *inputs,
-            smem=1, hbm=len(inputs), hbm_out=True, limit=LAYER_LIMIT,
-            scratch=scratch
-            + [pltpu.VMEM(tail.shape[-2:], BF), pltpu.SemaphoreType.DMA((13,))]
-            + [pltpu.VMEM(o.shape, BF) for o in out]
-            + [pltpu.SemaphoreType.DMA((4,))],
+            out, *inputs,
+            hbm=2, limit=LAYER_LIMIT, scratch=scratch,
         )
         if last:
             keys = out[0]
         else:
             state, coarse, halo, inner = out
+        if layer == 0:
+            gathered, state = lax.optimization_barrier((gathered, state))
+            gathered_other = lax.ppermute(gathered, "space", swap)
 
     twins = [[i, i + 1] for i in range(0, sections, 2)]
     keys = lax.all_gather(keys, "section", axis=0, axis_index_groups=twins)
-    own, near, far = call(deliver_kernel, (block, block, block), core, keys, decode_senders[0], smem=1)
+    own, near, far = call(deliver_kernel, (block, block, block), keys, decode_senders[0])
     far = gather_crossing(far)
     near = gather_pair(near)
     return call(
         decode_kernel,
         shape((samples, grid_rows, output_weight.shape[1])),
-        core, own, near, far, queries, decode_features[:, 0, 0, :], decode_edge_weight, vec(decode_bias),
+        own, near, far, queries, decode_features[:, 0, 0, :], decode_edge_weight, vec(decode_bias),
         decode_receivers[0], x, output_weight,
-        smem=1,
     )
 
 

time: 204 us -> 192 us (0.941)
  blocking collectives: 104 us -> 80.4 us
  starting transfers between devices: 30.3 us -> 43.8 us
  waiting for transfers between devices: 13.8 us -> 22.9 us
  Pallas kernels: 31.4 us -> 25.4 us
  local copies, waits for them, and re-layouts: 9.71 us -> 5.11 us
    all_to_all x1 -> x0, blocking collectives: 22.4 us -> none  [shards(): lax.all_to_all(coarse, 'space', 0, 0, tiled=True, axis_index_groups=same_...]
    all_to_all x3 -> x4, starting transfers between devices: 23.6 us -> 35 us  [shards(): lax.all_to_all(coarse, 'space', 0, 0, tiled=True, axis_index_groups=same_...]
    pallas_call x12, Pallas kernels: 31.4 us -> 25.4 us  [call(): pl.pallas_call(kernel, out_shape=out, in_specs=specs, out_specs=jax.tree....]
    all_to_all x3 -> x4, waiting for transfers between devices: 5.57 us -> 9.82 us  [shards(): lax.all_to_all(coarse, 'space', 0, 0, tiled=True, axis_index_groups=same_...]
    unnamed x68 -> x48, local copies, waits for them, and re-layouts: 5.63 us -> 2.3 us
    ppermute x0 -> x1, waiting for transfers between devices: none -> 2.72 us  [shards(): gathered_other = lax.ppermute(gathered[0], 'space', swap)]
    reshape x4, local copies, waits for them, and re-layouts: 2.82 us -> 0.23 us  [shards(): coarse = coarse.reshape(owners, latent)]
  transfers between devices with their start and end apart: 6 -> 8, of which waited for: 5 -> 7; matrix products, arithmetic and copies ran while one was open for 1% -> 0% of each run, Pallas kernels for 2% -> 2%
where the time goes in v3:
time: 192 us
  blocking collectives  80.4 us (42%)
  starting transfers between devices  43.8 us (23%)
  Pallas kernels  25.4 us (13%)
  waiting for transfers between devices  22.9 us (12%)
  between operations  13.8 us (7%)
  local copies, waits for them, and re-layouts  5.11 us (3%)
    all_gather x6, blocking collectives, gather_crossing(): return lax.all_gather(value, 'space', axis=0, axis_index_groups=crossings)  58.9 us
    all_to_all x4, starting transfers between devices, shards(): lax.all_to_all(coarse, 'space', 0, 0, tiled=True, axis_index_groups=same_...  35 us
    pallas_call x12, Pallas kernels, call(): pl.pallas_call(kernel, out_shape=out, in_specs=specs, out_specs=jax.tree....  25.4 us
    all_gather x8, blocking collectives, gather_pair(): return lax.all_gather(value, 'space', axis=0, axis_index_groups=pairs)  15.9 us
    all_to_all x4, waiting for transfers between devices, shards(): lax.all_to_all(coarse, 'space', 0, 0, tiled=True, axis_index_groups=same_...  9.82 us
    all_to_all x1, waiting for transfers between devices, shards(): parts = lax.all_to_all(parts, 'section', 0, 0, tiled=True)  9.31 us
    all_gather x1, blocking collectives, shards(): keys = lax.all_gather(keys, 'section', axis=0, axis_index_groups=twins)  5.64 us
    all_to_all x1, starting transfers between devices, shards(): parts = lax.all_to_all(parts, 'section', 0, 0, tiled=True)  4.82 us
  transfers between devices with their start and end apart: 8, of which 7 were waited for; matrix products, arithmetic and copies ran while one was open for 0% of the time, Pallas kernels for 2%

profile of v3, /device:TPU:2, one launch (start us, length us, event | category | flops | bytes accessed | tf_op | source)
XLA Modules:
  0.0 191.7 jit_solution(678376732891639216)
XLA Ops:
  6.6 2.2 %shard_map.235 = bf16[1088,512]{1,0:T(8,128)(2,1)} custom-call(f32[4,512]{1,0:T(4,128)} %bitcast.84, f32[2,512]{1,0:T(2,128)} %bitcast.86, f32[1,512]{1,0:T(1,128)} %gain_from.1, bf16[4,512,512]{2,1,0:T(8,128)(2,1)} %bitcast.78), custom_call_target="tpu_custom_call" | custom-call | flops 1000000 | bytes 1000000 | tf_op jit(solution)/shard_map/pallas_call | solution.py:79
  11.1 2.1 %all-gather.1 = bf16[256,512]{1,0:T(8,128)(2,1)S(1)} all-gather(bf16[128,512]{1,0:T(8,128)(2,1)S(1)} %get-tuple-element.38), channel_id=3, replica_groups={{0,1},{2,3},{4,5},{6,7},{8,9},{10,11},{12,13},{14,15},{16,17},{18,19},{..., dimensions={0}, use_global_device_ids=true | all-gather | bytes 393216 | tf_op jit(solution)/shard_map/all_gather | solution.py:363
  13.3 15.0 %all-gather.2 = bf16[256,512]{1,0:T(8,128)(2,1)S(1)} all-gather(bf16[128,512]{1,0:T(8,128)(2,1)S(1)} %get-tuple-element.39), channel_id=4, replica_groups={{1,2},{3,4},{5,6},{7,8},{9,10},{11,12},{13,14},{15,16},{17,18},{19,20},..., dimensions={0}, use_global_device_ids=true | all-gather | bytes 393216 | tf_op jit(solution)/shard_map/all_gather | solution.py:366
  29.7 4.8 %all-to-all-start = ((bf16[4,128,512]{2,1,0:T(8,128)(2,1)}), bf16[4,128,512]{2,1,0:T(8,128)(2,1)S(1)}, u32[]{:S(2)}, u32[]{:S(2)}) async-start(bf16[4,128,512]{2,1,0:T(8,128)(2,1)} %shard_map.237), calls=%async_computation | async-start | bytes 1048576 | tf_op jit(solution)/shard_map/all_to_all | solution.py:423
  37.4 9.3 %all-to-all-done.parts = bf16[4,128,512]{2,1,0:T(8,128)(2,1)S(1)} async-done(((bf16[4,128,512]{2,1,0:T(8,128)(2,1)}), bf16[4,128,512]{2,1,0:T(8,128)(2,1)S(1)}, u32[]{:S(2)}, u32[]{:S(2)}) %all-to-all-start) | async-done | bytes 524320 | tf_op jit(solution)/shard_map/all_to_all | solution.py:423
  49.7 9.4 %all-to-all-start.1 = ((bf16[64,2,512]{2,1,0:T(2,128)(2,1)}), bf16[64,2,512]{2,1,0:T(2,128)(2,1)S(1)}, u32[]{:S(2)}, u32[]{:S(2)}) async-start(bf16[64,2,512]{2,1,0:T(2,128)(2,1)} %get-tuple-element.42), calls=%async_computation.1 | async-start | bytes 262144 | tf_op jit(solution)/shard_map/all_to_all | solution.py:441
  59.0 8.9 %all-gather.5 = bf16[96,512]{1,0:T(8,128)(2,1)S(1)} all-gather(bf16[48,512]{1,0:T(8,128)(2,1)S(1)} %get-tuple-element.41), channel_id=7, replica_groups={{1,2},{3,4},{5,6},{7,8},{9,10},{11,12},{13,14},{15,16},{17,18},{19,20},..., dimensions={0}, use_global_device_ids=true | all-gather | bytes 147456 | tf_op jit(solution)/shard_map/all_gather | solution.py:366
  69.8 2.6 %all-to-all-done.1 = bf16[64,2,512]{2,1,0:T(2,128)(2,1)S(1)} async-done(((bf16[64,2,512]{2,1,0:T(2,128)(2,1)}), bf16[64,2,512]{2,1,0:T(2,128)(2,1)S(1)}, u32[]{:S(2)}, u32[]{:S(2)}) %all-to-all-start.1) | async-done | bytes 131104 | tf_op jit(solution)/shard_map/all_to_all | solution.py:441
  76.8 2.7 %collective-permute-done.refs_8_ = bf16[1088,512]{1,0:T(8,128)(2,1)S(1)} collective-permute-done((bf16[1088,512]{1,0:T(8,128)(2,1)S(1)}, bf16[1088,512]{1,0:T(8,128)(2,1)S(1)}, u32[]{:S(2)}, u32[]{:S(2)}) %collective-permute-start) | collective-permute-done | bytes 1114144 | tf_op jit(solution)/shard_map/ppermute | solution.py:446
  80.5 4.3 %shard_map.241 = (bf16[256,512]{1,0:T(8,128)(2,1)S(1)}, bf16[64,2,512]{2,1,0:T(2,128)(2,1)}, bf16[48,512]{1,0:T(8,128)(2,1)S(1)}, bf16[32,512]{1,0:T(8,128)(2,1)S(1)}) custom-call(bf16[256,512]{1,0:T(8,128)(2,1)S(1)} %all-gather.3.state.refs_0_, bf16[2,2,48,512]{3,2,1,0:T(8,128)(2,1)S(1)} %bitcast.63, bf16[32,512]{1,0:T(8,128)(2,1)S(1)} %get-tuple-element.45.refs_2_, ...), custom_call_target="tpu_custom_call" | custom-call | flops 1000000 | bytes 1000000 | tf_op jit(solution)/shard_map/pallas_call | solution.py:79
  86.9 12.5 %all-to-all-start.2 = ((bf16[64,2,512]{2,1,0:T(2,128)(2,1)}), bf16[64,2,512]{2,1,0:T(2,128)(2,1)S(1)}, u32[]{:S(2)}, u32[]{:S(2)}) async-start(bf16[64,2,512]{2,1,0:T(2,128)(2,1)} %get-tuple-element.53), calls=%async_computation.2 | async-start | bytes 262144 | tf_op jit(solution)/shard_map/all_to_all | solution.py:441
  99.4 9.1 %all-gather.7 = bf16[96,512]{1,0:T(8,128)(2,1)S(1)} all-gather(bf16[48,512]{1,0:T(8,128)(2,1)S(1)} %get-tuple-element.51), channel_id=9, replica_groups={{1,2},{3,4},{5,6},{7,8},{9,10},{11,12},{13,14},{15,16},{17,18},{19,20},..., dimensions={0}, use_global_device_ids=true | all-gather | bytes 147456 | tf_op jit(solution)/shard_map/all_gather | solution.py:366
  110.4 2.7 %all-to-all-done.2 = bf16[64,2,512]{2,1,0:T(2,128)(2,1)S(1)} async-done(((bf16[64,2,512]{2,1,0:T(2,128)(2,1)}), bf16[64,2,512]{2,1,0:T(2,128)(2,1)S(1)}, u32[]{:S(2)}, u32[]{:S(2)}) %all-to-all-start.2) | async-done | bytes 131104 | tf_op jit(solution)/shard_map/all_to_all | solution.py:441
  113.1 4.3 %shard_map.242 = (bf16[256,512]{1,0:T(8,128)(2,1)S(1)}, bf16[64,2,512]{2,1,0:T(2,128)(2,1)}, bf16[48,512]{1,0:T(8,128)(2,1)S(1)}, bf16[32,512]{1,0:T(8,128)(2,1)S(1)}) custom-call(bf16[256,512]{1,0:T(8,128)(2,1)S(1)} %get-tuple-element.50.refs_0_, bf16[2,2,48,512]{3,2,1,0:T(8,128)(2,1)S(1)} %bitcast.65, bf16[32,512]{1,0:T(8,128)(2,1)S(1)} %get-tuple-element.52.refs_2_, ...), custom_call_target="tpu_custom_call" | custom-call | flops 1000000 | bytes 1000000 | tf_op jit(solution)/shard_map/pallas_call | solution.py:79
  117.5 6.4 %all-to-all-start.3 = ((bf16[64,2,512]{2,1,0:T(2,128)(2,1)}), bf16[64,2,512]{2,1,0:T(2,128)(2,1)S(1)}, u32[]{:S(2)}, u32[]{:S(2)}) async-start(bf16[64,2,512]{2,1,0:T(2,128)(2,1)} %get-tuple-element.58), calls=%async_computation.3 | async-start | bytes 262144 | tf_op jit(solution)/shard_map/all_to_all | solution.py:441
  123.9 8.9 %all-gather.9 = bf16[96,512]{1,0:T(8,128)(2,1)S(1)} all-gather(bf16[48,512]{1,0:T(8,128)(2,1)S(1)} %get-tuple-element.56), channel_id=11, replica_groups={{1,2},{3,4},{5,6},{7,8},{9,10},{11,12},{13,14},{15,16},{17,18},{19,20},..., dimensions={0}, use_global_device_ids=true | all-gather | bytes 147456 | tf_op jit(solution)/shard_map/all_gather | solution.py:366
  134.9 2.4 %all-to-all-done.3 = bf16[64,2,512]{2,1,0:T(2,128)(2,1)S(1)} async-done(((bf16[64,2,512]{2,1,0:T(2,128)(2,1)}), bf16[64,2,512]{2,1,0:T(2,128)(2,1)S(1)}, u32[]{:S(2)}, u32[]{:S(2)}) %all-to-all-start.3) | async-done | bytes 131104 | tf_op jit(solution)/shard_map/all_to_all | solution.py:441
  137.4 4.4 %shard_map.243 = (bf16[256,512]{1,0:T(8,128)(2,1)S(1)}, bf16[64,2,512]{2,1,0:T(2,128)(2,1)}, bf16[48,512]{1,0:T(8,128)(2,1)S(1)}, bf16[32,512]{1,0:T(8,128)(2,1)S(1)}) custom-call(bf16[256,512]{1,0:T(8,128)(2,1)S(1)} %get-tuple-element.55.refs_0_, bf16[2,2,48,512]{3,2,1,0:T(8,128)(2,1)S(1)} %bitcast.66, bf16[32,512]{1,0:T(8,128)(2,1)S(1)} %get-tuple-element.57.refs_2_, ...), custom_call_target="tpu_custom_call" | custom-call | flops 1000000 | bytes 1000000 | tf_op jit(solution)/shard_map/pallas_call | solution.py:79
  141.8 6.8 %all-to-all-start.4 = ((bf16[64,2,512]{2,1,0:T(2,128)(2,1)}), bf16[64,2,512]{2,1,0:T(2,128)(2,1)S(1)}, u32[]{:S(2)}, u32[]{:S(2)}) async-start(bf16[64,2,512]{2,1,0:T(2,128)(2,1)} %get-tuple-element.62), calls=%async_computation.4 | async-start | bytes 262144 | tf_op jit(solution)/shard_map/all_to_all | solution.py:441
  148.8 8.7 %all-gather.11 = bf16[96,512]{1,0:T(8,128)(2,1)S(1)} all-gather(bf16[48,512]{1,0:T(8,128)(2,1)S(1)} %get-tuple-element.60), channel_id=13, replica_groups={{1,2},{3,4},{5,6},{7,8},{9,10},{11,12},{13,14},{15,16},{17,18},{19,20},..., dimensions={0}, use_global_device_ids=true | all-gather | bytes 147456 | tf_op jit(solution)/shard_map/all_gather | solution.py:366
  159.4 2.2 %all-to-all-done.4 = bf16[64,2,512]{2,1,0:T(2,128)(2,1)S(1)} async-done(((bf16[64,2,512]{2,1,0:T(2,128)(2,1)}), bf16[64,2,512]{2,1,0:T(2,128)(2,1)S(1)}, u32[]{:S(2)}, u32[]{:S(2)}) %all-to-all-start.4) | async-done | bytes 131104 | tf_op jit(solution)/shard_map/all_to_all | solution.py:441
  161.7 5.1 %shard_map.244 = bf16[128,512]{1,0:T(8,128)(2,1)S(1)} custom-call(bf16[256,512]{1,0:T(8,128)(2,1)S(1)} %get-tuple-element.59.refs_0_, bf16[2,2,48,512]{3,2,1,0:T(8,128)(2,1)S(1)} %bitcast.64, bf16[32,512]{1,0:T(8,128)(2,1)S(1)} %get-tuple-element.61.refs_2_, bf16[128,512]{1,0:T(8,128)(2,1)S(1)} %reshape.47.refs_3_, ...), custom_call_target="tpu_custom_call" | custom-call | flops 1000000 | bytes 1000000 | tf_op jit(solution)/shard_map/pallas_call | solution.py:79
  166.8 5.6 %all-gather.13 = bf16[256,512]{1,0:T(8,128)(2,1)S(1)} all-gather(bf16[128,512]{1,0:T(8,128)(2,1)S(1)} %shard_map.244), channel_id=15, replica_groups={{0,128},{256,384},{1,129},{257,385},{2,130},{258,386},{3,131},{259,387}..., dimensions={0}, use_global_device_ids=true | all-gather | bytes 393216 | tf_op jit(solution)/shard_map/all_gather | solution.py:469
  174.7 8.4 %all-gather.15 = bf16[256,512]{1,0:T(8,128)(2,1)S(1)} all-gather(bf16[128,512]{1,0:T(8,128)(2,1)S(1)} %get-tuple-element.65), channel_id=17, replica_groups={{1,2},{3,4},{5,6},{7,8},{9,10},{11,12},{13,14},{15,16},{17,18},{19,20},..., dimensions={0}, use_global_device_ids=true | all-gather | bytes 393216 | tf_op jit(solution)/shard_map/all_gather | solution.py:366
  (86 shorter events, 29.1 us)
Async XLA Ops:
  6.5 67.0 %all-gather.18.cloned.1.call-start = ((), (), s32[]{:S(2)}) async-start(), calls=%async_computation.5 | async-start | bytes 5570560 | tf_op jit(solution)/shard_map/all_gather | solution.py:385
  6.5 2.6 %copy-start.5 = (f32[512]{0:T(512)S(1)}, f32[512]{0:T(512)}, u32[]{:S(2)}) copy-start(f32[512]{0:T(512)} %param.27) | copy-start | bytes 6148
  6.6 2.6 %copy-start.9 = (s32[1,1,192]{2,1,0:T(1,128)S(1)}, s32[1,1,192]{2,1,0:T(1,128)}, u32[]{:S(2)}) copy-start(s32[1,1,192]{2,1,0:T(1,128)} %param.40) | copy-start | bytes 2308
  8.9 19.4 %copy-start.3 = (f32[4,512]{1,0:T(4,128)S(1)}, f32[4,512]{1,0:T(4,128)}, u32[]{:S(2)}) copy-start(f32[4,512]{1,0:T(4,128)} %weight.2) | copy-start | bytes 24580
  8.9 19.4 %copy-start.6 = (f32[512]{0:T(512)S(1)}, f32[512]{0:T(512)}, u32[]{:S(2)}) copy-start(f32[512]{0:T(512)} %param.30) | copy-start | bytes 6148
  8.9 19.4 %copy-start.11 = (s32[1,1,192]{2,1,0:T(1,128)S(1)}, s32[1,1,192]{2,1,0:T(1,128)}, u32[]{:S(2)}) copy-start(s32[1,1,192]{2,1,0:T(1,128)} %param.41) | copy-start | bytes 2308
  11.1 23.4 %copy-start.16 = (s32[1,64]{1,0:T(1,128)S(1)}, s32[1,64]{1,0:T(1,128)}, u32[]{:S(2)}) copy-start(s32[1,64]{1,0:T(1,128)} %param.43) | copy-start | bytes 772
  11.1 23.8 %copy-start.17 = (f32[4,1,448]{2,1,0:T(1,128)S(1)}, f32[4,1,448]{2,1,0:T(1,128)}, u32[]{:S(2)}) copy-start(f32[4,1,448]{2,1,0:T(1,128)} %param.46) | copy-start | bytes 21508
  11.1 23.8 %copy-start.20 = (s32[1,448]{1,0:T(1,128)S(1)}, s32[1,448]{1,0:T(1,128)}, u32[]{:S(2)}) copy-start(s32[1,448]{1,0:T(1,128)} %param.45) | copy-start | bytes 5380
  11.1 23.8 %copy-start.21 = (s32[1,448]{1,0:T(1,128)S(1)}, s32[1,448]{1,0:T(1,128)}, u32[]{:S(2)}) copy-start(s32[1,448]{1,0:T(1,128)} %param.44) | copy-start | bytes 5380
  11.1 35.6 %copy-start.7 = (f32[512]{0:T(512)S(1)}, f32[512]{0:T(512)}, u32[]{:S(2)}) copy-start(f32[512]{0:T(512)} %param.31) | copy-start | bytes 6148
  29.7 17.0 %all-to-all-start = ((bf16[4,128,512]{2,1,0:T(8,128)(2,1)}), bf16[4,128,512]{2,1,0:T(8,128)(2,1)S(1)}, u32[]{:S(2)}, u32[]{:S(2)}) async-start(bf16[4,128,512]{2,1,0:T(8,128)(2,1)} %shard_map.237), calls=%async_computation | async-start | bytes 1048576 | tf_op jit(solution)/shard_map/all_to_all | solution.py:423
  49.7 22.8 %all-to-all-start.1 = ((bf16[64,2,512]{2,1,0:T(2,128)(2,1)}), bf16[64,2,512]{2,1,0:T(2,128)(2,1)S(1)}, u32[]{:S(2)}, u32[]{:S(2)}) async-start(bf16[64,2,512]{2,1,0:T(2,128)(2,1)} %get-tuple-element.42), calls=%async_computation.1 | async-start | bytes 262144 | tf_op jit(solution)/shard_map/all_to_all | solution.py:441
  74.8 4.6 %collective-permute-start = (bf16[1088,512]{1,0:T(8,128)(2,1)S(1)}, bf16[1088,512]{1,0:T(8,128)(2,1)S(1)}, u32[]{:S(2)}, u32[]{:S(2)}) collective-permute-start(bf16[1088,512]{1,0:T(8,128)(2,1)S(1)} %slice_bitcast_fusion), channel_id=1, source_target_pairs={{0,1},{1,0},{2,3},{3,2},{4,5},{5,4},{6,7},{7,6},{8,9},{9,8},{10,11... | collective-permute-start | bytes 3342344 | tf_op jit(solution)/shard_map/ppermute | solution.py:446
  84.9 28.2 %collective-permute-start.1 = (bf16[4,1088,512]{2,1,0:T(8,128)(2,1)}, bf16[4,1088,512]{2,1,0:T(8,128)(2,1)}, u32[]{:S(2)}, u32[]{:S(2)}) collective-permute-start(bf16[4,1088,512]{2,1,0:T(8,128)(2,1)} %bitcast.3.refs_7_), channel_id=1, source_target_pairs={{0,1},{1,0},{2,3},{3,2},{4,5},{5,4},{6,7},{7,6},{8,9},{9,8},{10,11... | collective-permute-start | bytes 13369352 | tf_op jit(solution)/shard_map/ppermute | solution.py:466
  86.9 26.1 %all-to-all-start.2 = ((bf16[64,2,512]{2,1,0:T(2,128)(2,1)}), bf16[64,2,512]{2,1,0:T(2,128)(2,1)S(1)}, u32[]{:S(2)}, u32[]{:S(2)}) async-start(bf16[64,2,512]{2,1,0:T(2,128)(2,1)} %get-tuple-element.53), calls=%async_computation.2 | async-start | bytes 262144 | tf_op jit(solution)/shard_map/all_to_all | solution.py:441
  117.5 19.8 %all-to-all-start.3 = ((bf16[64,2,512]{2,1,0:T(2,128)(2,1)}), bf16[64,2,512]{2,1,0:T(2,128)(2,1)S(1)}, u32[]{:S(2)}, u32[]{:S(2)}) async-start(bf16[64,2,512]{2,1,0:T(2,128)(2,1)} %get-tuple-element.58), calls=%async_computation.3 | async-start | bytes 262144 | tf_op jit(solution)/shard_map/all_to_all | solution.py:441
  137.3 11.3 %copy-start.15 = (bf16[512,227]{0,1:T(8,128)(2,1)S(1)}, bf16[512,227]{0,1:T(8,128)(2,1)}, u32[]{:S(2)}) copy-start(bf16[512,227]{0,1:T(8,128)(2,1)} %param.39) | copy-start | bytes 697348
  137.3 11.4 %copy-start.19 = (f32[4,1,1,192]{3,2,1,0:T(1,128)S(1)}, f32[4,1,1,192]{3,2,1,0:T(1,128)}, u32[]{:S(2)}) copy-start(f32[4,1,1,192]{3,2,1,0:T(1,128)} %param.49) | copy-start | bytes 9220
  141.8 19.8 %all-to-all-start.4 = ((bf16[64,2,512]{2,1,0:T(2,128)(2,1)}), bf16[64,2,512]{2,1,0:T(2,128)(2,1)S(1)}, u32[]{:S(2)}, u32[]{:S(2)}) async-start(bf16[64,2,512]{2,1,0:T(2,128)(2,1)} %get-tuple-element.62), calls=%async_computation.4 | async-start | bytes 262144 | tf_op jit(solution)/shard_map/all_to_all | solution.py:441
  161.6 10.8 %copy-start.10 = (s32[1,1,192]{2,1,0:T(1,128)S(1)}, s32[1,1,192]{2,1,0:T(1,128)}, u32[]{:S(2)}) copy-start(s32[1,1,192]{2,1,0:T(1,128)} %param.47) | copy-start | bytes 2308
  161.7 21.5 %copy-start.4 = (f32[4,512]{1,0:T(4,128)S(1)}, f32[4,512]{1,0:T(4,128)}, u32[]{:S(2)}) copy-start(f32[4,512]{1,0:T(4,128)} %weight.3) | copy-start | bytes 24580
  161.7 21.5 %copy-start.8 = (f32[512]{0:T(512)S(1)}, f32[512]{0:T(512)}, u32[]{:S(2)}) copy-start(f32[512]{0:T(512)} %param.38) | copy-start | bytes 6148
  161.7 21.4 %copy-start.12 = (s32[1,1,192]{2,1,0:T(1,128)S(1)}, s32[1,1,192]{2,1,0:T(1,128)}, u32[]{:S(2)}) copy-start(s32[1,1,192]{2,1,0:T(1,128)} %param.48) | copy-start | bytes 2308
  (6 other events, 12.0 us)
Sparse Core Ops, SparseCore 0:
  9.5 64.0 all-gather.17

commit v4 on v3

--- a/solution.py
+++ b/solution.py
@@ -14,6 +14,7 @@
 EXTRA = 64
 NODE_BIAS, GAIN = 32, 35
 SMALL_LIMIT = 16 * 1024 * 1024
+FIRST_LIMIT = 51000000
 LAYER_LIMIT = 54000000
 PACK_LIMIT = 64_900_000
 
@@ -208,8 +209,12 @@
     ).astype(F32)
 
 
+def feature_rows(features):
+    return jnp.concatenate([features[c] for c in range(features.shape[0])], axis=0)
+
+
 def message_kernel(own, near, far, features, weight, bias, receivers, out):
-    edge = edge_term(features[...], weight[...]) + bias[...]
+    edge = edge_term(feature_rows(features), weight[...]) + bias[...]
     hot = hot_rows(receivers[...], ROWS)
     for sample in range(2):
         rows = arrived_rows(own, near, far, sample)
@@ -330,15 +335,17 @@
 
 
 def decode_kernel(own, near, far, queries, features, weight, bias, receivers, x, out_weight, out):
-    edge = edge_term(features[...], weight[...]) + bias[...]
+    edge = edge_term(feature_rows(features), weight[...]) + bias[...]
     hot = hot_rows(receivers[...], ROWS)
-    width = out_weight.shape[1]
+    width = out_weight.shape[0]
     for sample in range(2):
         at = pl.ds(sample * ROWS, ROWS)
         rows = arrived_rows(own, near, far, sample)
         hidden = silu(rows + dot_t(hot, queries[at]) + edge).astype(BF)
         total = dot(hot, hidden).astype(BF)
-        change = dot(total, out_weight[...])
+        change = lax.dot_general(
+            total, out_weight[...], (((1,), (1,)), ((), ())), preferred_element_type=F32
+        )
         out[sample] = (x[at, :width].astype(F32) + change).astype(BF)
 
 
@@ -418,7 +425,7 @@
     parts = call(
         message_kernel,
         shape((sections, ROWS, latent)),
-        own, near, far, encode_features[:, 0, 0, :], encode_edge_weight, vec(encode_bias), encode_receivers[0],
+        own, near, far, encode_features[:, 0], encode_edge_weight, vec(encode_bias), encode_receivers[0],
     )
     parts = lax.all_to_all(parts, "section", 0, 0, tiled=True)
     start = call(start_kernel, shape((ROWS, latent)), parts, vec(mesh_gain))
@@ -455,7 +462,7 @@
         out = call(
             functools.partial(layer_kernel, layer=layer, last=last),
             out, *inputs,
-            hbm=2, limit=LAYER_LIMIT, scratch=scratch,
+            hbm=2, limit=FIRST_LIMIT if layer == 0 else LAYER_LIMIT, scratch=scratch,
         )
         if last:
             keys = out[0]
@@ -473,8 +480,8 @@
     return call(
         decode_kernel,
         shape((samples, grid_rows, output_weight.shape[1])),
-        own, near, far, queries, decode_features[:, 0, 0, :], decode_edge_weight, vec(decode_bias),
-        decode_receivers[0], x, output_weight,
+        own, near, far, queries, decode_features[:, 0], decode_edge_weight, vec(decode_bias),
+        decode_receivers[0], x, output_weight.T,
     )
 
 

time: 192 us -> 192 us (level)
  no operation moved by 1% of the time
where the time goes in v4:
time: 192 us; the launch traced here: 191 us
  blocking collectives  80.5 us (42%)
  starting transfers between devices  43.7 us (23%)
  Pallas kernels  25.5 us (13%)
  waiting for transfers between devices  23.4 us (12%)
  between operations  13.8 us (7%)
  local copies, waits for them, and re-layouts  3.95 us (2%)
    all_gather x6, blocking collectives, gather_crossing(): return lax.all_gather(value, 'space', axis=0, axis_index_groups=crossings)  59 us
    all_to_all x4, starting transfers between devices, shards(): lax.all_to_all(coarse, 'space', 0, 0, tiled=True, axis_index_groups=same_...  35 us
    pallas_call x12, Pallas kernels, call(): pl.pallas_call(kernel, out_shape=out, in_specs=specs, out_specs=jax.tree....  25.5 us
    all_gather x8, blocking collectives, gather_pair(): return lax.all_gather(value, 'space', axis=0, axis_index_groups=pairs)  15.9 us
    all_to_all x4, waiting for transfers between devices, shards(): lax.all_to_all(coarse, 'space', 0, 0, tiled=True, axis_index_groups=same_...  10.3 us
    all_to_all x1, waiting for transfers between devices, shards(): parts = lax.all_to_all(parts, 'section', 0, 0, tiled=True)  9.3 us
    all_gather x1, blocking collectives, shards(): keys = lax.all_gather(keys, 'section', axis=0, axis_index_groups=twins)  5.64 us
    all_to_all x1, starting transfers between devices, shards(): parts = lax.all_to_all(parts, 'section', 0, 0, tiled=True)  4.83 us
  transfers between devices with their start and end apart: 8, of which 7 were waited for; matrix products, arithmetic and copies ran while one was open for 0% of the time, Pallas kernels for 2%

profile of v4, /device:TPU:2, one launch (start us, length us, event | category | flops | bytes accessed | tf_op | source)
XLA Modules:
  0.0 191.0 jit_solution(15274371728870030251)
XLA Ops:
  6.6 2.3 %shard_map.235 = bf16[1088,512]{1,0:T(8,128)(2,1)} custom-call(f32[4,512]{1,0:T(4,128)} %bitcast.82, f32[2,512]{1,0:T(2,128)} %bitcast.84, f32[1,512]{1,0:T(1,128)} %gain_from.1, bf16[4,512,512]{2,1,0:T(8,128)(2,1)} %bitcast.76), custom_call_target="tpu_custom_call" | custom-call | flops 1000000 | bytes 1000000 | tf_op jit(solution)/shard_map/pallas_call | solution.py:80
  11.1 2.1 %all-gather.1 = bf16[256,512]{1,0:T(8,128)(2,1)S(1)} all-gather(bf16[128,512]{1,0:T(8,128)(2,1)S(1)} %get-tuple-element.38), channel_id=3, replica_groups={{0,1},{2,3},{4,5},{6,7},{8,9},{10,11},{12,13},{14,15},{16,17},{18,19},{..., dimensions={0}, use_global_device_ids=true | all-gather | bytes 393216 | tf_op jit(solution)/shard_map/all_gather | solution.py:370
  13.3 15.0 %all-gather.2 = bf16[256,512]{1,0:T(8,128)(2,1)S(1)} all-gather(bf16[128,512]{1,0:T(8,128)(2,1)S(1)} %get-tuple-element.39), channel_id=4, replica_groups={{1,2},{3,4},{5,6},{7,8},{9,10},{11,12},{13,14},{15,16},{17,18},{19,20},..., dimensions={0}, use_global_device_ids=true | all-gather | bytes 393216 | tf_op jit(solution)/shard_map/all_gather | solution.py:373
  29.7 4.8 %all-to-all-start = ((bf16[4,128,512]{2,1,0:T(8,128)(2,1)}), bf16[4,128,512]{2,1,0:T(8,128)(2,1)S(1)}, u32[]{:S(2)}, u32[]{:S(2)}) async-start(bf16[4,128,512]{2,1,0:T(8,128)(2,1)} %shard_map.237), calls=%async_computation | async-start | bytes 1048576 | tf_op jit(solution)/shard_map/all_to_all | solution.py:430
  37.4 9.3 %all-to-all-done.parts = bf16[4,128,512]{2,1,0:T(8,128)(2,1)S(1)} async-done(((bf16[4,128,512]{2,1,0:T(8,128)(2,1)}), bf16[4,128,512]{2,1,0:T(8,128)(2,1)S(1)}, u32[]{:S(2)}, u32[]{:S(2)}) %all-to-all-start) | async-done | bytes 524320 | tf_op jit(solution)/shard_map/all_to_all | solution.py:430
  49.7 9.3 %all-to-all-start.1 = ((bf16[64,2,512]{2,1,0:T(2,128)(2,1)}), bf16[64,2,512]{2,1,0:T(2,128)(2,1)S(1)}, u32[]{:S(2)}, u32[]{:S(2)}) async-start(bf16[64,2,512]{2,1,0:T(2,128)(2,1)} %get-tuple-element.42), calls=%async_computation.1 | async-start | bytes 262144 | tf_op jit(solution)/shard_map/all_to_all | solution.py:448
  59.0 8.9 %all-gather.5 = bf16[96,512]{1,0:T(8,128)(2,1)S(1)} all-gather(bf16[48,512]{1,0:T(8,128)(2,1)S(1)} %get-tuple-element.41), channel_id=7, replica_groups={{1,2},{3,4},{5,6},{7,8},{9,10},{11,12},{13,14},{15,16},{17,18},{19,20},..., dimensions={0}, use_global_device_ids=true | all-gather | bytes 147456 | tf_op jit(solution)/shard_map/all_gather | solution.py:373
  69.8 2.6 %all-to-all-done.1 = bf16[64,2,512]{2,1,0:T(2,128)(2,1)S(1)} async-done(((bf16[64,2,512]{2,1,0:T(2,128)(2,1)}), bf16[64,2,512]{2,1,0:T(2,128)(2,1)S(1)}, u32[]{:S(2)}, u32[]{:S(2)}) %all-to-all-start.1) | async-done | bytes 131104 | tf_op jit(solution)/shard_map/all_to_all | solution.py:448
  76.8 2.7 %collective-permute-done.refs_8_ = bf16[1088,512]{1,0:T(8,128)(2,1)S(1)} collective-permute-done((bf16[1088,512]{1,0:T(8,128)(2,1)S(1)}, bf16[1088,512]{1,0:T(8,128)(2,1)S(1)}, u32[]{:S(2)}, u32[]{:S(2)}) %collective-permute-start) | collective-permute-done | bytes 1114144 | tf_op jit(solution)/shard_map/ppermute | solution.py:453
  79.5 4.3 %shard_map.241 = (bf16[256,512]{1,0:T(8,128)(2,1)S(1)}, bf16[64,2,512]{2,1,0:T(2,128)(2,1)}, bf16[48,512]{1,0:T(8,128)(2,1)S(1)}, bf16[32,512]{1,0:T(8,128)(2,1)S(1)}) custom-call(bf16[256,512]{1,0:T(8,128)(2,1)S(1)} %all-gather.3.state.refs_0_, bf16[2,2,48,512]{3,2,1,0:T(8,128)(2,1)S(1)} %bitcast.60, bf16[32,512]{1,0:T(8,128)(2,1)S(1)} %get-tuple-element.45.refs_2_, ...), custom_call_target="tpu_custom_call" | custom-call | flops 1000000 | bytes 1000000 | tf_op jit(solution)/shard_map/pallas_call | solution.py:80
  85.8 12.5 %all-to-all-start.2 = ((bf16[64,2,512]{2,1,0:T(2,128)(2,1)}), bf16[64,2,512]{2,1,0:T(2,128)(2,1)S(1)}, u32[]{:S(2)}, u32[]{:S(2)}) async-start(bf16[64,2,512]{2,1,0:T(2,128)(2,1)} %get-tuple-element.53), calls=%async_computation.2 | async-start | bytes 262144 | tf_op jit(solution)/shard_map/all_to_all | solution.py:448
  98.2 9.0 %all-gather.7 = bf16[96,512]{1,0:T(8,128)(2,1)S(1)} all-gather(bf16[48,512]{1,0:T(8,128)(2,1)S(1)} %get-tuple-element.51), channel_id=9, replica_groups={{1,2},{3,4},{5,6},{7,8},{9,10},{11,12},{13,14},{15,16},{17,18},{19,20},..., dimensions={0}, use_global_device_ids=true | all-gather | bytes 147456 | tf_op jit(solution)/shard_map/all_gather | solution.py:373
  109.2 2.7 %all-to-all-done.2 = bf16[64,2,512]{2,1,0:T(2,128)(2,1)S(1)} async-done(((bf16[64,2,512]{2,1,0:T(2,128)(2,1)}), bf16[64,2,512]{2,1,0:T(2,128)(2,1)S(1)}, u32[]{:S(2)}, u32[]{:S(2)}) %all-to-all-start.2) | async-done | bytes 131104 | tf_op jit(solution)/shard_map/all_to_all | solution.py:448
  112.0 4.4 %shard_map.242 = (bf16[256,512]{1,0:T(8,128)(2,1)S(1)}, bf16[64,2,512]{2,1,0:T(2,128)(2,1)}, bf16[48,512]{1,0:T(8,128)(2,1)S(1)}, bf16[32,512]{1,0:T(8,128)(2,1)S(1)}) custom-call(bf16[256,512]{1,0:T(8,128)(2,1)S(1)} %get-tuple-element.50.refs_0_, bf16[2,2,48,512]{3,2,1,0:T(8,128)(2,1)S(1)} %bitcast.62, bf16[32,512]{1,0:T(8,128)(2,1)S(1)} %get-tuple-element.52.refs_2_, ...), custom_call_target="tpu_custom_call" | custom-call | flops 1000000 | bytes 1000000 | tf_op jit(solution)/shard_map/pallas_call | solution.py:80
  116.4 6.4 %all-to-all-start.3 = ((bf16[64,2,512]{2,1,0:T(2,128)(2,1)}), bf16[64,2,512]{2,1,0:T(2,128)(2,1)S(1)}, u32[]{:S(2)}, u32[]{:S(2)}) async-start(bf16[64,2,512]{2,1,0:T(2,128)(2,1)} %get-tuple-element.58), calls=%async_computation.3 | async-start | bytes 262144 | tf_op jit(solution)/shard_map/all_to_all | solution.py:448
  122.7 8.9 %all-gather.9 = bf16[96,512]{1,0:T(8,128)(2,1)S(1)} all-gather(bf16[48,512]{1,0:T(8,128)(2,1)S(1)} %get-tuple-element.56), channel_id=11, replica_groups={{1,2},{3,4},{5,6},{7,8},{9,10},{11,12},{13,14},{15,16},{17,18},{19,20},..., dimensions={0}, use_global_device_ids=true | all-gather | bytes 147456 | tf_op jit(solution)/shard_map/all_gather | solution.py:373
  133.7 2.4 %all-to-all-done.3 = bf16[64,2,512]{2,1,0:T(2,128)(2,1)S(1)} async-done(((bf16[64,2,512]{2,1,0:T(2,128)(2,1)}), bf16[64,2,512]{2,1,0:T(2,128)(2,1)S(1)}, u32[]{:S(2)}, u32[]{:S(2)}) %all-to-all-start.3) | async-done | bytes 131104 | tf_op jit(solution)/shard_map/all_to_all | solution.py:448
  136.2 4.4 %shard_map.243 = (bf16[256,512]{1,0:T(8,128)(2,1)S(1)}, bf16[64,2,512]{2,1,0:T(2,128)(2,1)}, bf16[48,512]{1,0:T(8,128)(2,1)S(1)}, bf16[32,512]{1,0:T(8,128)(2,1)S(1)}) custom-call(bf16[256,512]{1,0:T(8,128)(2,1)S(1)} %get-tuple-element.55.refs_0_, bf16[2,2,48,512]{3,2,1,0:T(8,128)(2,1)S(1)} %bitcast.63, bf16[32,512]{1,0:T(8,128)(2,1)S(1)} %get-tuple-element.57.refs_2_, ...), custom_call_target="tpu_custom_call" | custom-call | flops 1000000 | bytes 1000000 | tf_op jit(solution)/shard_map/pallas_call | solution.py:80
  140.5 6.8 %all-to-all-start.4 = ((bf16[64,2,512]{2,1,0:T(2,128)(2,1)}), bf16[64,2,512]{2,1,0:T(2,128)(2,1)S(1)}, u32[]{:S(2)}, u32[]{:S(2)}) async-start(bf16[64,2,512]{2,1,0:T(2,128)(2,1)} %get-tuple-element.62), calls=%async_computation.4 | async-start | bytes 262144 | tf_op jit(solution)/shard_map/all_to_all | solution.py:448
  147.4 8.9 %all-gather.11 = bf16[96,512]{1,0:T(8,128)(2,1)S(1)} all-gather(bf16[48,512]{1,0:T(8,128)(2,1)S(1)} %get-tuple-element.60), channel_id=13, replica_groups={{1,2},{3,4},{5,6},{7,8},{9,10},{11,12},{13,14},{15,16},{17,18},{19,20},..., dimensions={0}, use_global_device_ids=true | all-gather | bytes 147456 | tf_op jit(solution)/shard_map/all_gather | solution.py:373
  158.2 2.6 %all-to-all-done.4 = bf16[64,2,512]{2,1,0:T(2,128)(2,1)S(1)} async-done(((bf16[64,2,512]{2,1,0:T(2,128)(2,1)}), bf16[64,2,512]{2,1,0:T(2,128)(2,1)S(1)}, u32[]{:S(2)}, u32[]{:S(2)}) %all-to-all-start.4) | async-done | bytes 131104 | tf_op jit(solution)/shard_map/all_to_all | solution.py:448
  160.9 5.2 %shard_map.244 = bf16[128,512]{1,0:T(8,128)(2,1)S(1)} custom-call(bf16[256,512]{1,0:T(8,128)(2,1)S(1)} %get-tuple-element.59.refs_0_, bf16[2,2,48,512]{3,2,1,0:T(8,128)(2,1)S(1)} %bitcast.61, bf16[32,512]{1,0:T(8,128)(2,1)S(1)} %get-tuple-element.61.refs_2_, bf16[128,512]{1,0:T(8,128)(2,1)S(1)} %reshape.47.refs_3_, ...), custom_call_target="tpu_custom_call" | custom-call | flops 1000000 | bytes 1000000 | tf_op jit(solution)/shard_map/pallas_call | solution.py:80
  166.1 5.6 %all-gather.13 = bf16[256,512]{1,0:T(8,128)(2,1)S(1)} all-gather(bf16[128,512]{1,0:T(8,128)(2,1)S(1)} %shard_map.244), channel_id=15, replica_groups={{0,128},{256,384},{1,129},{257,385},{2,130},{258,386},{3,131},{259,387}..., dimensions={0}, use_global_device_ids=true | all-gather | bytes 393216 | tf_op jit(solution)/shard_map/all_gather | solution.py:476
  174.1 8.4 %all-gather.15 = bf16[256,512]{1,0:T(8,128)(2,1)S(1)} all-gather(bf16[128,512]{1,0:T(8,128)(2,1)S(1)} %get-tuple-element.65), channel_id=17, replica_groups={{1,2},{3,4},{5,6},{7,8},{9,10},{11,12},{13,14},{15,16},{17,18},{19,20},..., dimensions={0}, use_global_device_ids=true | all-gather | bytes 393216 | tf_op jit(solution)/shard_map/all_gather | solution.py:373
  (81 shorter events, 27.8 us)
Async XLA Ops:
  6.5 67.0 %all-gather.18.cloned.1.call-start = ((), (), s32[]{:S(2)}) async-start(), calls=%async_computation.5 | async-start | bytes 5570560 | tf_op jit(solution)/shard_map/all_gather | solution.py:392
  6.5 2.6 %copy-start.12 = (s32[1,1,192]{2,1,0:T(1,128)S(1)}, s32[1,1,192]{2,1,0:T(1,128)}, u32[]{:S(2)}) copy-start(s32[1,1,192]{2,1,0:T(1,128)} %param.40) | copy-start | bytes 2308
  8.9 19.4 %copy-start.4 = (f32[4,512]{1,0:T(4,128)S(1)}, f32[4,512]{1,0:T(4,128)}, u32[]{:S(2)}) copy-start(f32[4,512]{1,0:T(4,128)} %weight.2) | copy-start | bytes 24580
  8.9 19.4 %copy-start.6 = (f32[4,1,1,192]{3,2,1,0:T(1,128)S(1)}, f32[4,1,1,192]{3,2,1,0:T(1,128)}, u32[]{:S(2)}) copy-start(f32[4,1,1,192]{3,2,1,0:T(1,128)} %param.42) | copy-start | bytes 9220
  8.9 19.4 %copy-start.9 = (f32[512]{0:T(512)S(1)}, f32[512]{0:T(512)}, u32[]{:S(2)}) copy-start(f32[512]{0:T(512)} %param.30) | copy-start | bytes 6148
  8.9 19.4 %copy-start.14 = (s32[1,1,192]{2,1,0:T(1,128)S(1)}, s32[1,1,192]{2,1,0:T(1,128)}, u32[]{:S(2)}) copy-start(s32[1,1,192]{2,1,0:T(1,128)} %param.41) | copy-start | bytes 2308
  11.1 23.4 %copy-start.17 = (s32[1,64]{1,0:T(1,128)S(1)}, s32[1,64]{1,0:T(1,128)}, u32[]{:S(2)}) copy-start(s32[1,64]{1,0:T(1,128)} %param.43) | copy-start | bytes 772
  11.1 23.8 %copy-start.18 = (f32[4,1,448]{2,1,0:T(1,128)S(1)}, f32[4,1,448]{2,1,0:T(1,128)}, u32[]{:S(2)}) copy-start(f32[4,1,448]{2,1,0:T(1,128)} %param.46) | copy-start | bytes 21508
  11.1 23.8 %copy-start.19 = (s32[1,448]{1,0:T(1,128)S(1)}, s32[1,448]{1,0:T(1,128)}, u32[]{:S(2)}) copy-start(s32[1,448]{1,0:T(1,128)} %param.45) | copy-start | bytes 5380
  11.1 23.8 %copy-start.20 = (s32[1,448]{1,0:T(1,128)S(1)}, s32[1,448]{1,0:T(1,128)}, u32[]{:S(2)}) copy-start(s32[1,448]{1,0:T(1,128)} %param.44) | copy-start | bytes 5380
  11.1 35.6 %copy-start.10 = (f32[512]{0:T(512)S(1)}, f32[512]{0:T(512)}, u32[]{:S(2)}) copy-start(f32[512]{0:T(512)} %param.31) | copy-start | bytes 6148
  29.7 17.0 %all-to-all-start = ((bf16[4,128,512]{2,1,0:T(8,128)(2,1)}), bf16[4,128,512]{2,1,0:T(8,128)(2,1)S(1)}, u32[]{:S(2)}, u32[]{:S(2)}) async-start(bf16[4,128,512]{2,1,0:T(8,128)(2,1)} %shard_map.237), calls=%async_computation | async-start | bytes 1048576 | tf_op jit(solution)/shard_map/all_to_all | solution.py:430
  49.7 22.7 %all-to-all-start.1 = ((bf16[64,2,512]{2,1,0:T(2,128)(2,1)}), bf16[64,2,512]{2,1,0:T(2,128)(2,1)S(1)}, u32[]{:S(2)}, u32[]{:S(2)}) async-start(bf16[64,2,512]{2,1,0:T(2,128)(2,1)} %get-tuple-element.42), calls=%async_computation.1 | async-start | bytes 262144 | tf_op jit(solution)/shard_map/all_to_all | solution.py:448
  74.8 4.6 %collective-permute-start = (bf16[1088,512]{1,0:T(8,128)(2,1)S(1)}, bf16[1088,512]{1,0:T(8,128)(2,1)S(1)}, u32[]{:S(2)}, u32[]{:S(2)}) collective-permute-start(bf16[1088,512]{1,0:T(8,128)(2,1)S(1)} %slice_bitcast_fusion), channel_id=1, source_target_pairs={{0,1},{1,0},{2,3},{3,2},{4,5},{5,4},{6,7},{7,6},{8,9},{9,8},{10,11... | collective-permute-start | bytes 3342344 | tf_op jit(solution)/shard_map/ppermute | solution.py:453
  83.8 28.1 %collective-permute-start.1 = (bf16[4,1088,512]{2,1,0:T(8,128)(2,1)}, bf16[4,1088,512]{2,1,0:T(8,128)(2,1)}, u32[]{:S(2)}, u32[]{:S(2)}) collective-permute-start(bf16[4,1088,512]{2,1,0:T(8,128)(2,1)} %bitcast.3.refs_7_), channel_id=1, source_target_pairs={{0,1},{1,0},{2,3},{3,2},{4,5},{5,4},{6,7},{7,6},{8,9},{9,8},{10,11... | collective-permute-start | bytes 13369352 | tf_op jit(solution)/shard_map/ppermute | solution.py:473
  85.8 26.2 %all-to-all-start.2 = ((bf16[64,2,512]{2,1,0:T(2,128)(2,1)}), bf16[64,2,512]{2,1,0:T(2,128)(2,1)S(1)}, u32[]{:S(2)}, u32[]{:S(2)}) async-start(bf16[64,2,512]{2,1,0:T(2,128)(2,1)} %get-tuple-element.53), calls=%async_computation.2 | async-start | bytes 262144 | tf_op jit(solution)/shard_map/all_to_all | solution.py:448
  116.4 19.8 %all-to-all-start.3 = ((bf16[64,2,512]{2,1,0:T(2,128)(2,1)}), bf16[64,2,512]{2,1,0:T(2,128)(2,1)S(1)}, u32[]{:S(2)}, u32[]{:S(2)}) async-start(bf16[64,2,512]{2,1,0:T(2,128)(2,1)} %get-tuple-element.58), calls=%async_computation.3 | async-start | bytes 262144 | tf_op jit(solution)/shard_map/all_to_all | solution.py:448
  140.5 20.2 %all-to-all-start.4 = ((bf16[64,2,512]{2,1,0:T(2,128)(2,1)}), bf16[64,2,512]{2,1,0:T(2,128)(2,1)S(1)}, u32[]{:S(2)}, u32[]{:S(2)}) async-start(bf16[64,2,512]{2,1,0:T(2,128)(2,1)} %get-tuple-element.62), calls=%async_computation.4 | async-start | bytes 262144 | tf_op jit(solution)/shard_map/all_to_all | solution.py:448
  160.8 10.9 %copy-start.13 = (s32[1,1,192]{2,1,0:T(1,128)S(1)}, s32[1,1,192]{2,1,0:T(1,128)}, u32[]{:S(2)}) copy-start(s32[1,1,192]{2,1,0:T(1,128)} %param.47) | copy-start | bytes 2308
  160.9 21.6 %copy-start.3 = (bf16[512,227]{0,1:T(8,128)(2,1)S(1)}, bf16[512,227]{0,1:T(8,128)(2,1)}, u32[]{:S(2)}) copy-start(bf16[512,227]{0,1:T(8,128)(2,1)} %param.39) | copy-start | bytes 697348
  160.9 21.6 %copy-start.5 = (f32[4,512]{1,0:T(4,128)S(1)}, f32[4,512]{1,0:T(4,128)}, u32[]{:S(2)}) copy-start(f32[4,512]{1,0:T(4,128)} %weight.3) | copy-start | bytes 24580
  160.9 21.6 %copy-start.7 = (f32[4,1,1,192]{3,2,1,0:T(1,128)S(1)}, f32[4,1,1,192]{3,2,1,0:T(1,128)}, u32[]{:S(2)}) copy-start(f32[4,1,1,192]{3,2,1,0:T(1,128)} %param.49) | copy-start | bytes 9220
  160.9 21.6 %copy-start.11 = (f32[512]{0:T(512)S(1)}, f32[512]{0:T(512)}, u32[]{:S(2)}) copy-start(f32[512]{0:T(512)} %param.38) | copy-start | bytes 6148
  160.9 21.6 %copy-start.15 = (s32[1,1,192]{2,1,0:T(1,128)S(1)}, s32[1,1,192]{2,1,0:T(1,128)}, u32[]{:S(2)}) copy-start(s32[1,1,192]{2,1,0:T(1,128)} %param.48) | copy-start | bytes 2308
  (5 other events, 11.1 us)
Sparse Core Ops, SparseCore 0:
  9.5 64.0 all-gather.17
